TPU v7x, 32 devices: a whole 2x2x4 slice. The times are simulated.
32 devices in a mesh: seq: 8 (over z, y), head: 4 (over x, core).
Axes of the slice: x: 2, y: 2, z: 4, core: 2. Of those that a mesh axis runs over, the one named last changes fastest.
Arguments:
- queries: bfloat16 [4096, 8192], P('seq', 'head'), may hold values from -4 to 4
- key_vecs: bfloat16 [4096, 8192], P('seq', 'head'), may hold values from -4 to 4
- value_vecs: bfloat16 [4096, 8192], P('seq', 'head'), may hold values from -6 to 6
- log_decay: float32 [4096, 64], P('seq', 'head'), may hold values from -3 to 0, as said below
- norm_gain: float32 [8192], P('head'), may hold values from 0.1 to 1.9
- cotangent: bfloat16 [4096, 8192], P('seq', 'head'), may hold values from -6 to 6
Outputs:
- attended: bfloat16 [4096, 8192], P('seq', 'head')
- grad_queries: bfloat16 [4096, 8192], P('seq', 'head')
- grad_keys: bfloat16 [4096, 8192], P('seq', 'head')
- grad_values: bfloat16 [4096, 8192], P('seq', 'head')
Inputs may be any that keep to these rules, and one draw needn't show every extreme that they name: `log_decay`: every entry is negative.
All inputs are finite; a program needn't handle non-finite values.
Results may differ from a plain program's by a relative error of at most 0.0051.
Values sent between devices are 32-bit elements; how exact they have to be, the bound alone decides.
No kernel may reach another device: no remote copies, remote signals or barrier semaphores. Data moves between devices by JAX's collectives and lax.ppermute only.
A program may use at most 128 MiB of HBM per device.

v0:
```python
import functools

import jax
import jax.numpy as jnp
from jax import lax
from jax.experimental import pallas as pl
from jax.experimental.pallas import tpu as pltpu
from jax.sharding import PartitionSpec as P

HEAD_DIM = 128
BLOCK = 512
CHUNKS = 2
TILE = 256
epsilon = 1e-06
f32 = jnp.float32
bf16 = jnp.bfloat16

NN = (((1,), (0,)), ((), ()))
NT = (((1,), (1,)), ((), ()))
TN = (((0,), (0,)), ((), ()))


def dot(a, b, dims=NN):
    return lax.dot_general(a, b, dims, preferred_element_type=f32)


def halves(x):
    high = x.astype(bf16)
    return high, (x - high.astype(f32)).astype(bf16)


def column(row):
    return jnp.transpose(jnp.broadcast_to(row, (HEAD_DIM, row.shape[1])))


def wide(col, width):
    return jnp.concatenate([col] * (width // HEAD_DIM), axis=1)


def cumulative(decay):
    length = decay.shape[1]
    first = decay.astype(bf16)
    rest = decay - first.astype(f32)
    second = rest.astype(bf16)
    third = (rest - second.astype(f32)).astype(bf16)
    upto = lax.broadcasted_iota(jnp.int32, (length, length), 0) <= lax.broadcasted_iota(
        jnp.int32, (length, length), 1
    )
    upto = jnp.where(upto, 1.0, 0.0).astype(bf16)
    return dot(first, upto) + dot(second, upto) + dot(third, upto)


def trail_row(row):
    return jnp.exp(row[:, -1:] - row)


def outer_sum(left, scale_row, right):
    scaled = jnp.transpose(left.astype(f32)) * scale_row
    high, low = halves(scaled)
    return dot(high, right) + dot(low, right)


def cols(j):
    return slice(j * HEAD_DIM, (j + 1) * HEAD_DIM)


class Part:
    def __init__(self, chunk, slot, half):
        self.chunk, self.slot, self.half = chunk, slot, half
        self.steps = 2 if half % 4 == 0 else 1
        self.per_step = half // self.steps

    def group(self, info):
        return info[0][0] if self.slot == "mine" else 1 - info[0][0]

    def head(self, info, j):
        return (2 * self.chunk + self.group(info)) * self.half + pl.program_id(0) * self.per_step + j

    def row(self, cumul_ref, info, j):
        return cumul_ref[pl.ds(self.head(info, j), 1), :]

    def wide_cols(self, info, j):
        return pl.ds(pl.multiple_of(self.head(info, j) * HEAD_DIM, HEAD_DIM), HEAD_DIM)

    def state_rows(self, j):
        start = (pl.program_id(0) * self.per_step + j) * HEAD_DIM
        return pl.ds(pl.multiple_of(start, HEAD_DIM), HEAD_DIM)


def store_decays(part, info, cumul_ref, out_ref):
    for j in range(part.per_step):
        row = part.row(cumul_ref, info, j)
        place = part.half * HEAD_DIM + pl.program_id(0) * part.per_step + j
        out_ref[pl.ds(place, 1), :] = jnp.broadcast_to(jnp.exp(row[:, -1:]), (1, HEAD_DIM))


def pieces_kernel(part, info, key_ref, value_ref, cumul_ref, out_ref):
    for j in range(part.per_step):
        row = part.row(cumul_ref, info, j)
        at = part.wide_cols(info, j)
        out_ref[part.state_rows(j), :] = outer_sum(key_ref[:, at], trail_row(row), value_ref[:, at])
    store_decays(part, info, cumul_ref, out_ref)


def first_pieces_kernel(part, info, key_ref, value_ref, decay_ref, out_ref, cumul_ref):
    @pl.when(pl.program_id(0) == 0)
    def _():
        cumul_ref[...] = cumulative(decay_ref[...])

    pieces_kernel(part, info, key_ref, value_ref, cumul_ref, out_ref)


def inner_kernel(part, info, query_ref, key_ref, value_ref, cumul_ref, out_ref):
    for j in range(part.per_step):
        row = part.row(cumul_ref, info, j)
        col = column(row)
        at = part.wide_cols(info, j)
        query, key, value = query_ref[:, at], key_ref[:, at], value_ref[:, at]
        for top in range(0, BLOCK, TILE):
            end = top + TILE
            scores = dot(query[top:end], key[:end], NT)
            spread = wide(col[top:end], end) - row[:, :end]
            causal = lax.broadcasted_iota(jnp.int32, (TILE, end), 0) + top >= (
                lax.broadcasted_iota(jnp.int32, (TILE, end), 1)
            )
            weights = (scores * jnp.exp(jnp.where(causal, spread, -1e30))).astype(bf16)
            out_ref[top:end, part.state_rows(j)] = dot(weights, value[:end])


def output_kernel(
    part, info, inner_ref, query_ref, cot_ref, gain_ref, cumul_ref, state_ref, before_ref,
    out_ref, sums_ref, square_ref, product_ref,
):
    step = pl.program_id(0)
    squares = jnp.zeros((BLOCK, HEAD_DIM), f32)
    products = jnp.zeros((BLOCK, HEAD_DIM), f32)
    for j in range(part.per_step):
        lead = jnp.exp(column(part.row(cumul_ref, info, j)))
        high, low = halves(state_ref[part.state_rows(j), :])
        at, here = part.wide_cols(info, j), part.state_rows(j)
        query = query_ref[:, at]
        out = inner_ref[:, here] + lead * (dot(query, high) + dot(query, low))
        out_ref[:, here] = out
        squares += out * out
        products += cot_ref[:, at].astype(f32) * gain_ref[:, at] * out

    @pl.when(step == 0)
    def _():
        square_ref[...] = squares
        product_ref[...] = products

    @pl.when(step > 0)
    def _():
        square_ref[...] += squares
        product_ref[...] += products

    @pl.when(step == part.steps - 1)
    def _():
        rows = lax.broadcasted_iota(jnp.int32, (8, HEAD_DIM), 0)
        total = before_ref[...]
        for place, ref in ((0, square_ref), (1, product_ref)):
            pick = jnp.where(rows == place, 1.0, 0.0).astype(bf16)
            high, low = halves(ref[...])
            total += dot(pick, high, NT) + dot(pick, low, NT)
        sums_ref[...] = total


def grad_kernel(features, part, info, out_ref, cot_ref, gain_ref, query_ref, cumul_ref, *refs):
    shares, (attended_ref, grad_ref, piece_ref) = refs[:-3], refs[-3:]
    sums = shares[0][...]
    for share in shares[1:]:
        sums = sums + share[...]
    inverse = lax.rsqrt(sums[0:1] / features + epsilon)
    mean_term = inverse * sums[1:2] / features
    inverse_col, mean_col = column(inverse), column(mean_term)
    for j in range(part.per_step):
        at, here = part.wide_cols(info, j), part.state_rows(j)
        gain = gain_ref[:, at]
        normed = out_ref[:, here] * inverse_col
        attended_ref[:, cols(j)] = (normed * gain).astype(bf16)
        scaled_grad = cot_ref[:, at].astype(f32) * gain
        grad = (inverse_col * (scaled_grad - normed * mean_col)).astype(bf16)
        grad_ref[:, here] = grad
        row = part.row(cumul_ref, info, j)
        piece_ref[part.state_rows(j), :] = outer_sum(query_ref[:, at], jnp.exp(row), grad)
    store_decays(part, info, cumul_ref, piece_ref)


def backward_kernel(
    part, info, query_ref, key_ref, value_ref, grad_ref, cumul_ref, state_ref,
    grad_query_ref, inner_key_ref, inner_value_ref,
):
    for j in range(part.per_step):
        row = part.row(cumul_ref, info, j)
        col = column(row)
        at, here = part.wide_cols(info, j), part.state_rows(j)
        query, key = query_ref[:, at], key_ref[:, at]
        value, grad = value_ref[:, at], grad_ref[:, here]
        high, low = halves(state_ref[part.state_rows(j), :])
        outer = jnp.exp(col) * (dot(grad, high, NT) + dot(grad, low, NT))
        for top in range(0, BLOCK, TILE):
            end = top + TILE
            scores = dot(key[top:end], query[top:], NT)
            grad_scores = dot(value[top:end], grad[top:], NT)
            spread = row[:, top:] - wide(col[top:end], BLOCK - top)
            causal = lax.broadcasted_iota(jnp.int32, spread.shape, 0) <= (
                lax.broadcasted_iota(jnp.int32, spread.shape, 1)
            )
            decays = jnp.exp(jnp.where(causal, spread, -1e30))
            weights = (scores * decays).astype(bf16)
            grad_weights = (grad_scores * decays).astype(bf16)
            inner_value_ref[top:end, here] = dot(weights, grad[top:])
            inner_key_ref[top:end, here] = dot(grad_weights, query[top:])
            inner_query = dot(grad_weights, key[top:end], TN)
            outer = inner_query + outer if top == 0 else jnp.concatenate(
                [outer[:top], outer[top:] + inner_query], axis=0
            )
        grad_query_ref[:, cols(j)] = outer.astype(bf16)


def final_kernel(
    part, info, inner_key_ref, inner_value_ref, key_ref, value_ref, cumul_ref, state_ref,
    grad_key_ref, grad_value_ref,
):
    for j in range(part.per_step):
        trail = column(trail_row(part.row(cumul_ref, info, j)))
        high, low = halves(state_ref[part.state_rows(j), :])
        at, here = part.wide_cols(info, j), part.state_rows(j)
        key, value = key_ref[:, at], value_ref[:, at]
        grad_key_ref[:, cols(j)] = (
            inner_key_ref[:, here] + trail * (dot(value, high, NT) + dot(value, low, NT))
        ).astype(bf16)
        grad_value_ref[:, cols(j)] = (
            inner_value_ref[:, here] + trail * (dot(key, high) + dot(key, low))
        ).astype(bf16)


def ordered(is_first, half, j, keep_ref, got_ref):
    rows = slice(j * HEAD_DIM, (j + 1) * HEAD_DIM)
    place = slice(half * HEAD_DIM + j, half * HEAD_DIM + j + 1)
    keep, got = keep_ref[rows, :], got_ref[rows, :]
    keep_decay, got_decay = keep_ref[place, :], got_ref[place, :]
    return (
        jnp.where(is_first, keep, got),
        jnp.where(is_first, got, keep),
        jnp.where(is_first, keep_decay, got_decay),
        jnp.where(is_first, got_decay, keep_decay),
    )


def scan_position(places, forward, info):
    member, pair = info[0][0], info[1][0]
    if forward:
        return member == 0, pair
    return member == 1, places - 1 - pair


def hop_kernel(half, p, position, info, keep_ref, got_ref, *refs):
    arrived, out_ref = refs[:-1], refs[-1]
    is_first, place = position(info)

    @pl.when(place == p)
    def _():
        for j in range(half):
            first, second, first_decay, second_decay = ordered(is_first, half, j, keep_ref, got_ref)
            value = second_decay * first + second
            for arrived_ref in arrived:
                value += (first_decay * second_decay) * arrived_ref[cols(j), :]
            out_ref[cols(j), :] = value


def last_kernel(half, position, info, keep_ref, got_ref, *refs):
    arrived, (mine_ref, send_ref) = refs[:-2], refs[-2:]
    is_first, place = position(info)
    for p in range(len(arrived) + 1):

        @pl.when(place == p)
        def _():
            for j in range(half):
                first, _, first_decay, _ = ordered(is_first, half, j, keep_ref, got_ref)
                if p == 0:
                    before, after = jnp.zeros_like(first), first
                else:
                    before = arrived[p - 1][cols(j), :]
                    after = first_decay * before + first
                mine_ref[cols(j), :] = jnp.where(is_first, before, after)
                send_ref[cols(j), :] = jnp.where(is_first, after, before)


def on_device(queries, key_vecs, value_vecs, log_decay, norm_gain, cotangent):
    tokens, width = queries.shape
    assert tokens == BLOCK
    heads = width // HEAD_DIM
    half = heads // (2 * CHUNKS)
    head_count = lax.axis_size("head")
    features = width * head_count
    places = lax.axis_size("seq") // 2
    my_index = lax.axis_index("seq")
    member, pair = my_index % 2, my_index // 2
    gain = norm_gain.reshape(1, width)

    any_spec = pl.BlockSpec(memory_space=pl.ANY)
    wide_state = jax.ShapeDtypeStruct((half * HEAD_DIM + 8, HEAD_DIM), f32)
    state = jax.ShapeDtypeStruct((half * HEAD_DIM, HEAD_DIM), f32)
    whole = jax.ShapeDtypeStruct((tokens, width), bf16)
    local = jax.ShapeDtypeStruct((tokens, half * HEAD_DIM), f32)
    local_low = jax.ShapeDtypeStruct((tokens, half * HEAD_DIM), bf16)
    sums_shape = jax.ShapeDtypeStruct((8, tokens), f32)
    info = (member.astype(jnp.int32).reshape(1), pair.astype(jnp.int32).reshape(1))

    def run(kernel, grid, ins, outs, scratch=(), after=(), aliases=None, cost=1.0):
        used = len(ins)
        after = [x for i, x in enumerate(after) if not any(x is y for y in after[:i])]

        def body(member_ref, pair_ref, *refs):
            kernel((member_ref, pair_ref), *refs[:used], *refs[used + len(after):])

        return pl.pallas_call(
            body,
            out_shape=[shape for shape, _ in outs],
            grid_spec=pltpu.PrefetchScalarGridSpec(
                num_scalar_prefetch=2,
                grid=(grid,),
                in_specs=[spec for _, spec in ins] + [any_spec] * len(after),
                out_specs=[spec for _, spec in outs],
                scratch_shapes=list(scratch),
            ),
            input_output_aliases=aliases or {},
            compiler_params=pltpu.CompilerParams(vmem_limit_bytes=24 * 1024 * 1024),
            cost_estimate=pl.CostEstimate(
                flops=int(cost * 1e9), bytes_accessed=int(cost * 2.5e6), transcendentals=0
            ),
        )(*info, *[array for array, _ in ins], *after)

    def fixed(shape):
        return pl.BlockSpec(shape, lambda i, *info: (0,) * len(shape))

    def plain(array):
        return array, fixed(array.shape)

    def give(shape):
        return shape, fixed(shape.shape)

    class Views(Part):
        def full_spec(self):
            return pl.BlockSpec(
                (tokens, self.per_step * HEAD_DIM),
                lambda i, *info: (0, (2 * self.chunk + self.group(info)) * self.steps + i),
            )

        def call(self, kernel, ins, outs, **options):
            return run(functools.partial(kernel, self), self.steps, ins, outs, **options)

    mine_parts = [Views(c, "mine", half) for c in range(CHUNKS)]
    their_parts = [Views(c, "theirs", half) for c in range(CHUNKS)]

    swap = [(2 * p + m, 2 * p + 1 - m) for p in range(places) for m in (0, 1)]

    def chain(make_piece, forward, early, filler, on_mine):
        position = functools.partial(scan_position, places, forward)

        def device(place, m):
            return 2 * (place if forward else places - 1 - place) + m

        received, last = [], ()
        for c in range(CHUNKS):
            sent = make_piece(their_parts[c], last)
            received.append(lax.ppermute(sent, "seq", swap))
            last = (sent,)
        keeps = []
        for c in range(CHUNKS):
            keeps.append(make_piece(mine_parts[c], last))
            last = (keeps[-1],)
        for work in early:
            last = (work(last),)
        arrived, mine, theirs = {}, [], []
        for p in range(places - 1):
            pairs = [(device(p, m), device(p + 1, m)) for m in (0, 1)]
            for c in range(CHUNKS):
                ins = [plain(keeps[c]), plain(received[c])]
                if p > 0:
                    ins.append(plain(arrived[c, p]))
                value, = run(
                    functools.partial(hop_kernel, half, p, position), 1, ins, [give(state)],
                    after=last, cost=0.3,
                )
                arrived[c, p + 1] = lax.ppermute(value, "seq", pairs)
                last = (value,)
            if filler:
                last = (filler.pop(0)(last),)
        for c in range(CHUNKS):
            ins = [plain(keeps[c]), plain(received[c])]
            ins += [plain(arrived[c, p]) for p in range(1, places)]
            own, send = run(
                functools.partial(last_kernel, half, position), 1, ins, [give(state)] * 2,
                after=last, cost=0.3,
            )
            theirs.append(lax.ppermute(send, "seq", swap))
            mine.append(own)
            last = (send,)
            filler.append(functools.partial(on_mine, c, own))
            last = (filler.pop(0)(last),)
        while filler:
            last = (filler.pop(0)(last),)
        return mine, theirs, last

    held_cumul = []

    def forward_piece(part, after):
        if not held_cumul:
            piece, cumul = part.call(
                first_pieces_kernel,
                [plain(key_vecs), plain(value_vecs), plain(log_decay.T)],
                [give(wide_state), give(jax.ShapeDtypeStruct((heads, tokens), f32))], cost=1.0,
            )
            held_cumul.append(cumul)
            return piece
        cumul = held_cumul[0]
        return part.call(
            pieces_kernel, [plain(key_vecs), plain(value_vecs), plain(cumul)],
            [give(wide_state)], after=after, cost=1.0,
        )[0]

    inner, outs = {}, {}

    def cumul_in():
        return plain(held_cumul[0])

    state_sums = [jnp.zeros(sums_shape.shape, f32)]

    def inner_work(part, after):
        inner[part], = part.call(
            inner_kernel,
            [plain(queries), plain(key_vecs), plain(value_vecs), cumul_in()],
            [give(local)], after=after, cost=2.2,
        )
        return inner[part]

    def output_work(part, before, after):
        outs[part], sums = part.call(
            output_kernel,
            [plain(inner[part]), plain(queries), plain(cotangent), plain(gain),
             cumul_in(), plain(before), plain(state_sums[0])],
            [give(local), give(sums_shape)],
            scratch=[pltpu.VMEM((tokens, HEAD_DIM), f32)] * 2, after=after, cost=1.4,
        )
        state_sums[0] = sums
        return sums

    inner_order = [part for c in range(CHUNKS) for part in (mine_parts[c], their_parts[c])]
    works = [functools.partial(inner_work, part) for part in inner_order]
    mine, theirs, last = chain(
        forward_piece, True, works[:1], works[1:],
        lambda c, own, after: output_work(mine_parts[c], own, after),
    )
    for c in range(CHUNKS):
        last = (output_work(their_parts[c], theirs[c], last),)

    sums = state_sums[0]
    shares = [sums] + [
        lax.ppermute(sums, "head", [(i, (i + k) % head_count) for i in range(head_count)])
        for k in range(1, head_count)
    ]

    attended, grad_queries, grad_keys, grad_values = [], [], [], []
    grads, inner_grads = {}, {}

    def target(held):
        return tuple(held[-1:])

    def backward_piece(part, after):
        before = target(attended)
        whole_out, grads[part], piece = part.call(
            functools.partial(grad_kernel, features),
            [plain(outs[part]), plain(cotangent), plain(gain), plain(queries),
             cumul_in()] + [plain(share) for share in shares],
            [(whole, part.full_spec()), give(local_low), give(wide_state)],
            after=before + tuple(after), aliases={7 + head_count: 0} if before else None, cost=2.0,
        )
        attended.append(whole_out)
        return piece

    def backward_work(part, before, after):
        held = target(grad_queries)
        whole_out, *inner_grads[part] = part.call(
            backward_kernel,
            [plain(queries), plain(key_vecs), plain(value_vecs),
             plain(grads[part]), cumul_in(), plain(before)],
            [(whole, part.full_spec()), give(local), give(local)],
            after=held + tuple(after), aliases={8: 0} if held else None, cost=4.3,
        )
        grad_queries.append(whole_out)
        return inner_grads[part][0]

    def final_work(part, before, after):
        held = target(grad_keys) + target(grad_values)
        whole_key, whole_value = part.call(
            final_kernel,
            [plain(inner_grads[part][0]), plain(inner_grads[part][1]),
             plain(key_vecs), plain(value_vecs), cumul_in(), plain(before)],
            [(whole, part.full_spec())] * 2,
            after=held + tuple(after), aliases={8: 0, 9: 1} if held else None, cost=2.0,
        )
        grad_keys.append(whole_key)
        grad_values.append(whole_value)
        return whole_key

    works = []
    for c in range(CHUNKS):
        works.append(functools.partial(backward_work, mine_parts[c], mine[c]))
        works.append(functools.partial(backward_work, their_parts[c], theirs[c]))
    mine_after, theirs_after, last = chain(
        backward_piece, False, [], works,
        lambda c, own, after: final_work(mine_parts[c], own, after),
    )
    for c in range(CHUNKS):
        final_work(their_parts[c], theirs_after[c], last)
        last = ()
    return attended[-1], grad_queries[-1], grad_keys[-1], grad_values[-1]


def solution(mesh):
    return jax.shard_map(
        on_device,
        mesh=mesh,
        in_specs=(
            P("seq", "head"),
            P("seq", "head"),
            P("seq", "head"),
            P("seq", "head"),
            P("head"),
            P("seq", "head"),
        ),
        out_specs=(P("seq", "head"), P("seq", "head"), P("seq", "head"), P("seq", "head")),
        check_vma=False,
    )
```

profile of v0, /device:TPU:0, one launch (start us, length us, event | category | flops | bytes accessed | tf_op | source)
XLA Modules:
  0.0 114.1 jit_solution(18259876005818360318)
XLA Ops:
  0.7 1.6 %copy-done.2 = bf16[512,2048]{1,0:T(8,128)(2,1)S(1)} copy-done((bf16[512,2048]{1,0:T(8,128)(2,1)S(1)}, bf16[512,2048]{1,0:T(8,128)(2,1)}, u32[]{:S(2)}) %copy-start.2) | copy-done | bytes 2097176
  2.2 1.6 %copy-done.4 = bf16[512,2048]{1,0:T(8,128)(2,1)S(1)} copy-done((bf16[512,2048]{1,0:T(8,128)(2,1)S(1)}, bf16[512,2048]{1,0:T(8,128)(2,1)}, u32[]{:S(2)}) %copy-start.4) | copy-done | bytes 2097176
  5.7 3.0 %collective-permute-start.1 = (f32[520,128]{1,0:T(8,128)S(1)}, f32[520,128]{1,0:T(8,128)S(1)}, u32[]{:S(2)}, u32[]{:S(2)}) collective-permute-start(f32[520,128]{1,0:T(8,128)S(1)} %get-tuple-element.55.refs_3_), channel_id=1, source_target_pairs={{0,4},{4,0},{8,12},{12,8},{16,20},{20,16},{24,28},{28,24},{1,5},{5... | collective-permute-start | bytes 798728 | tf_op jit(solution)/shard_map/ppermute | solution.py:368
  12.0 1.9 %shard_map.97.refs_2_.refs_0_ = f32[512,512]{1,0:T(8,128)S(1)} custom-call(s32[1]{0:T(128)} %bitcast.member_ref, s32[1]{0:T(128)} %bitcast.1.pair_ref, bf16[512,2048]{1,0:T(8,128)(2,1)S(1)} %copy-done.1, bf16[512,2048]{1,0:T(8,128)(2,1)S(1)} %copy-done.2, bf16[512,2048]{1,0:T(8,128)(2,1)S(1)} %copy-done.4, ...), custom_call_target="tpu_custom_call" | custom-call | flops 2200000000 | bytes 5500000 | tf_op jit(solution)/shard_map/pallas_call | solution.py:318
  13.9 2.0 %collective-permute-done.1.refs_1_ = f32[520,128]{1,0:T(8,128)S(1)} collective-permute-done((f32[520,128]{1,0:T(8,128)S(1)}, f32[520,128]{1,0:T(8,128)S(1)}, u32[]{:S(2)}, u32[]{:S(2)}) %collective-permute-start.1) | collective-permute-done | bytes 266272 | tf_op jit(solution)/shard_map/ppermute | solution.py:368
  16.0 4.0 %collective-permute-start.3 = (f32[512,128]{1,0:T(8,128)S(1)}, f32[512,128]{1,0:T(8,128)S(1)}, u32[]{:S(2)}, u32[]{:S(2)}) collective-permute-start(f32[512,128]{1,0:T(8,128)S(1)} %shard_map.98.refs_2_), channel_id=1, source_target_pairs={{0,8},{4,12},{1,9},{5,13},{2,10},{6,14},{3,11},{7,15}} | collective-permute-start | bytes 786440 | tf_op jit(solution)/shard_map/ppermute | solution.py:387
  20.9 3.6 %collective-permute-start.2 = (f32[512,128]{1,0:T(8,128)S(1)}, f32[512,128]{1,0:T(8,128)S(1)}, u32[]{:S(2)}, u32[]{:S(2)}) collective-permute-start(f32[512,128]{1,0:T(8,128)S(1)} %shard_map.99.refs_4_), channel_id=1, source_target_pairs={{0,8},{4,12},{1,9},{5,13},{2,10},{6,14},{3,11},{7,15}} | collective-permute-start | bytes 786440 | tf_op jit(solution)/shard_map/ppermute | solution.py:387
  24.5 1.9 %shard_map.100.refs_3_.refs_0_ = f32[512,512]{1,0:T(8,128)S(1)} custom-call(s32[1]{0:T(128)} %bitcast.member_ref, s32[1]{0:T(128)} %bitcast.1.pair_ref, bf16[512,2048]{1,0:T(8,128)(2,1)S(1)} %copy-done.1, bf16[512,2048]{1,0:T(8,128)(2,1)S(1)} %copy-done.3, bf16[512,2048]{1,0:T(8,128)(2,1)S(1)} %copy-done.4, ...), custom_call_target="tpu_custom_call" | custom-call | flops 2200000000 | bytes 5500000 | tf_op jit(solution)/shard_map/pallas_call | solution.py:318
  27.3 2.1 %collective-permute-done.2.refs_2_ = f32[512,128]{1,0:T(8,128)S(1)} collective-permute-done((f32[512,128]{1,0:T(8,128)S(1)}, f32[512,128]{1,0:T(8,128)S(1)}, u32[]{:S(2)}, u32[]{:S(2)}) %collective-permute-start.2) | collective-permute-done | bytes 262176 | tf_op jit(solution)/shard_map/ppermute | solution.py:387
  30.1 1.9 %shard_map.103.refs_3_.refs_0_ = f32[512,512]{1,0:T(8,128)S(1)} custom-call(s32[1]{0:T(128)} %bitcast.member_ref, s32[1]{0:T(128)} %bitcast.1.pair_ref, bf16[512,2048]{1,0:T(8,128)(2,1)S(1)} %copy-done.1, bf16[512,2048]{1,0:T(8,128)(2,1)S(1)} %copy-done.3, bf16[512,2048]{1,0:T(8,128)(2,1)S(1)} %copy-done.5, ...), custom_call_target="tpu_custom_call" | custom-call | flops 2200000000 | bytes 5500000 | tf_op jit(solution)/shard_map/pallas_call | solution.py:318
  33.5 1.9 %shard_map.106.refs_5_.refs_0_ = f32[512,512]{1,0:T(8,128)S(1)} custom-call(s32[1]{0:T(128)} %bitcast.member_ref, s32[1]{0:T(128)} %bitcast.1.pair_ref, bf16[512,2048]{1,0:T(8,128)(2,1)S(1)} %copy-done.1, bf16[512,2048]{1,0:T(8,128)(2,1)S(1)} %copy-done.3, bf16[512,2048]{1,0:T(8,128)(2,1)S(1)} %copy-done.5, ...), custom_call_target="tpu_custom_call" | custom-call | flops 2200000000 | bytes 5500000 | tf_op jit(solution)/shard_map/pallas_call | solution.py:318
  35.5 1.6 %collective-permute-start.9 = (f32[512,128]{1,0:T(8,128)S(1)}, f32[512,128]{1,0:T(8,128)S(1)}, u32[]{:S(2)}, u32[]{:S(2)}) collective-permute-start(f32[512,128]{1,0:T(8,128)S(1)} %get-tuple-element.57.refs_7_), channel_id=1, source_target_pairs={{0,4},{4,0},{8,12},{12,8},{16,20},{20,16},{24,28},{28,24},{1,5},{5... | collective-permute-start | bytes 786440 | tf_op jit(solution)/shard_map/ppermute | solution.py:398
  40.9 3.9 %collective-permute-done.9.refs_5_ = f32[512,128]{1,0:T(8,128)S(1)} collective-permute-done((f32[512,128]{1,0:T(8,128)S(1)}, f32[512,128]{1,0:T(8,128)S(1)}, u32[]{:S(2)}, u32[]{:S(2)}) %collective-permute-start.9) | collective-permute-done | bytes 262176 | tf_op jit(solution)/shard_map/ppermute | solution.py:398
  45.9 1.8 %collective-permute-done.8.refs_5_ = f32[512,128]{1,0:T(8,128)S(1)} collective-permute-done((f32[512,128]{1,0:T(8,128)S(1)}, f32[512,128]{1,0:T(8,128)S(1)}, u32[]{:S(2)}, u32[]{:S(2)}) %collective-permute-start.8) | collective-permute-done | bytes 262176 | tf_op jit(solution)/shard_map/ppermute | solution.py:398
  50.6 2.1 %collective-permute-done.11.refs_7_ = f32[8,512]{1,0:T(8,128)S(1)} collective-permute-done((f32[8,512]{1,0:T(8,128)S(1)}, f32[8,512]{1,0:T(8,128)S(1)}, u32[]{:S(2)}, u32[]{:S(2)}) %collective-permute-start.11) | collective-permute-done | bytes 16416 | tf_op jit(solution)/shard_map/ppermute | solution.py:461
  53.5 1.7 %shard_map.113 = (bf16[512,2048]{1,0:T(8,128)(2,1)}, bf16[512,512]{1,0:T(8,128)(2,1)S(1)}, f32[520,128]{1,0:T(8,128)S(1)}) custom-call(s32[1]{0:T(128)} %bitcast.member_ref, s32[1]{0:T(128)} %bitcast.1.pair_ref, f32[512,512]{1,0:T(8,128)S(1)} %get-tuple-element.67.refs_0_, bf16[512,2048]{1,0:T(8,128)(2,1)S(1)} %copy-done, f32[1,2048]{1,0:T(1,128)S(1)} %bitcast.8, ...), custom_call_target="tpu_custom_call" | custom-call | flops 2000000000 | bytes 5000000 | tf_op jit(solution)/shard_map/pallas_call | solution.py:318
  55.2 1.5 %collective-permute-start.14 = (f32[520,128]{1,0:T(8,128)S(1)}, f32[520,128]{1,0:T(8,128)S(1)}, u32[]{:S(2)}, u32[]{:S(2)}) collective-permute-start(f32[520,128]{1,0:T(8,128)S(1)} %get-tuple-element.69.refs_10_), channel_id=1, source_target_pairs={{0,4},{4,0},{8,12},{12,8},{16,20},{20,16},{24,28},{28,24},{1,5},{5... | collective-permute-start | bytes 798728 | tf_op jit(solution)/shard_map/ppermute | solution.py:368
  56.7 1.7 %shard_map.114 = (bf16[512,2048]{1,0:T(8,128)(2,1)}, bf16[512,512]{1,0:T(8,128)(2,1)S(1)}, f32[520,128]{1,0:T(8,128)S(1)}) custom-call(s32[1]{0:T(128)} %bitcast.member_ref, s32[1]{0:T(128)} %bitcast.1.pair_ref, f32[512,512]{1,0:T(8,128)S(1)} %get-tuple-element.66.refs_0_, bf16[512,2048]{1,0:T(8,128)(2,1)S(1)} %copy-done, ...), custom_call_target="tpu_custom_call", output_to_operand_aliasing={{0}: (11, {})} | custom-call | flops 2000000000 | bytes 5000000 | tf_op jit(solution)/shard_map/pallas_call | solution.py:318
  59.0 1.7 %shard_map.115 = (bf16[512,2048]{1,0:T(8,128)(2,1)}, bf16[512,512]{1,0:T(8,128)(2,1)S(1)}, f32[520,128]{1,0:T(8,128)S(1)}) custom-call(s32[1]{0:T(128)} %bitcast.member_ref, s32[1]{0:T(128)} %bitcast.1.pair_ref, f32[512,512]{1,0:T(8,128)S(1)} %get-tuple-element.65.refs_0_, bf16[512,2048]{1,0:T(8,128)(2,1)S(1)} %copy-done, ...), custom_call_target="tpu_custom_call", output_to_operand_aliasing={{0}: (11, {})} | custom-call | flops 2000000000 | bytes 5000000 | tf_op jit(solution)/shard_map/pallas_call | solution.py:318
  60.7 1.7 %shard_map.116 = (bf16[512,2048]{1,0:T(8,128)(2,1)}, bf16[512,512]{1,0:T(8,128)(2,1)S(1)}, f32[520,128]{1,0:T(8,128)S(1)}) custom-call(s32[1]{0:T(128)} %bitcast.member_ref, s32[1]{0:T(128)} %bitcast.1.pair_ref, f32[512,512]{1,0:T(8,128)S(1)} %get-tuple-element.61.refs_0_, bf16[512,2048]{1,0:T(8,128)(2,1)S(1)} %copy-done, ...), custom_call_target="tpu_custom_call", output_to_operand_aliasing={{0}: (11, {})} | custom-call | flops 2000000000 | bytes 5000000 | tf_op jit(solution)/shard_map/pallas_call | solution.py:318
  62.4 2.2 %collective-permute-done.14.refs_1_ = f32[520,128]{1,0:T(8,128)S(1)} collective-permute-done((f32[520,128]{1,0:T(8,128)S(1)}, f32[520,128]{1,0:T(8,128)S(1)}, u32[]{:S(2)}, u32[]{:S(2)}) %collective-permute-start.14) | collective-permute-done | bytes 266272 | tf_op jit(solution)/shard_map/ppermute | solution.py:368
  65.2 2.5 %collective-permute-done.13.refs_1_ = f32[520,128]{1,0:T(8,128)S(1)} collective-permute-done((f32[520,128]{1,0:T(8,128)S(1)}, f32[520,128]{1,0:T(8,128)S(1)}, u32[]{:S(2)}, u32[]{:S(2)}) %collective-permute-start.13) | collective-permute-done | bytes 266272 | tf_op jit(solution)/shard_map/ppermute | solution.py:368
  68.4 3.9 %shard_map.119 = (bf16[512,2048]{1,0:T(8,128)(2,1)}, f32[512,512]{1,0:T(8,128)S(1)}, f32[512,512]{1,0:T(8,128)S(1)}) custom-call(s32[1]{0:T(128)} %bitcast.member_ref, s32[1]{0:T(128)} %bitcast.1.pair_ref, bf16[512,2048]{1,0:T(8,128)(2,1)S(1)} %copy-done.1, bf16[512,2048]{1,0:T(8,128)(2,1)S(1)} %copy-done.3, bf16[512,2048]{1,0:T(8,128)(2,1)S(1)} %copy-done.5, ...), custom_call_target="tpu_custom_call" | custom-call | flops 4300000256 | bytes 10750000 | tf_op jit(solution)/shard_map/pallas_call | solution.py:318
  73.8 4.0 %shard_map.122 = (bf16[512,2048]{1,0:T(8,128)(2,1)}, f32[512,512]{1,0:T(8,128)S(1)}, f32[512,512]{1,0:T(8,128)S(1)}) custom-call(s32[1]{0:T(128)} %bitcast.member_ref, s32[1]{0:T(128)} %bitcast.1.pair_ref, bf16[512,2048]{1,0:T(8,128)(2,1)S(1)} %copy-done.1, bf16[512,2048]{1,0:T(8,128)(2,1)S(1)} %copy-done.3, ...), custom_call_target="tpu_custom_call", output_to_operand_aliasing={{0}: (8, {})} | custom-call | flops 4300000256 | bytes 10750000 | tf_op jit(solution)/shard_map/pallas_call | solution.py:318
  80.3 4.0 %shard_map.125 = (bf16[512,2048]{1,0:T(8,128)(2,1)}, f32[512,512]{1,0:T(8,128)S(1)}, f32[512,512]{1,0:T(8,128)S(1)}) custom-call(s32[1]{0:T(128)} %bitcast.member_ref, s32[1]{0:T(128)} %bitcast.1.pair_ref, bf16[512,2048]{1,0:T(8,128)(2,1)S(1)} %copy-done.1, bf16[512,2048]{1,0:T(8,128)(2,1)S(1)} %copy-done.3, ...), custom_call_target="tpu_custom_call", output_to_operand_aliasing={{0}: (8, {})} | custom-call | flops 4300000256 | bytes 10750000 | tf_op jit(solution)/shard_map/pallas_call | solution.py:318
  84.3 16.0 %collective-permute-done.19.refs_4_ = f32[512,128]{1,0:T(8,128)S(1)} collective-permute-done((f32[512,128]{1,0:T(8,128)S(1)}, f32[512,128]{1,0:T(8,128)S(1)}, u32[]{:S(2)}, u32[]{:S(2)}) %collective-permute-start.19) | collective-permute-done | bytes 262176 | tf_op jit(solution)/shard_map/ppermute | solution.py:387
  100.4 1.6 %collective-permute-start.22 = (f32[512,128]{1,0:T(8,128)S(1)}, f32[512,128]{1,0:T(8,128)S(1)}, u32[]{:S(2)}, u32[]{:S(2)}) collective-permute-start(f32[512,128]{1,0:T(8,128)S(1)} %get-tuple-element.86.refs_7_), channel_id=1, source_target_pairs={{0,4},{4,0},{8,12},{12,8},{16,20},{20,16},{24,28},{28,24},{1,5},{5... | collective-permute-start | bytes 786440 | tf_op jit(solution)/shard_map/ppermute | solution.py:398
  102.0 3.9 %shard_map.127 = (bf16[512,2048]{1,0:T(8,128)(2,1)}, f32[512,512]{1,0:T(8,128)S(1)}, f32[512,512]{1,0:T(8,128)S(1)}) custom-call(s32[1]{0:T(128)} %bitcast.member_ref, s32[1]{0:T(128)} %bitcast.1.pair_ref, bf16[512,2048]{1,0:T(8,128)(2,1)S(1)} %copy-done.1, bf16[512,2048]{1,0:T(8,128)(2,1)S(1)} %copy-done.3, ...), custom_call_target="tpu_custom_call", output_to_operand_aliasing={{0}: (8, {})} | custom-call | flops 4300000256 | bytes 10750000 | tf_op jit(solution)/shard_map/pallas_call | solution.py:318
  106.6 1.8 %shard_map.129 = (bf16[512,2048]{1,0:T(8,128)(2,1)}, bf16[512,2048]{1,0:T(8,128)(2,1)}) custom-call(s32[1]{0:T(128)} %bitcast.member_ref, s32[1]{0:T(128)} %bitcast.1.pair_ref, f32[512,512]{1,0:T(8,128)S(1)} %get-tuple-element.81.refs_3_.refs_0_, f32[512,512]{1,0:T(8,128)S(1)} %get-tuple-element.94.refs_1_, bf16[512,2048]{1,0:T(8,128)(2,1)S(1)} %copy-done.3, ...), custom_call_target="tpu_custom_call" | custom-call | flops 2000000000 | bytes 5000000 | tf_op jit(solution)/shard_map/pallas_call | solution.py:318
  108.3 1.8 %shard_map.130 = (bf16[512,2048]{1,0:T(8,128)(2,1)}, bf16[512,2048]{1,0:T(8,128)(2,1)}) custom-call(s32[1]{0:T(128)} %bitcast.member_ref, s32[1]{0:T(128)} %bitcast.1.pair_ref, f32[512,512]{1,0:T(8,128)S(1)} %get-tuple-element.85.refs_5_.refs_0_, f32[512,512]{1,0:T(8,128)S(1)} %get-tuple-element.92.refs_1_, ...), custom_call_target="tpu_custom_call", output_to_operand_aliasing={{0}: (8, {}), {1}: (9, {})} | custom-call | flops 2000000000 | bytes 5000000 | tf_op jit(solution)/shard_map/pallas_call | solution.py:318
  110.1 1.8 %shard_map.131 = (bf16[512,2048]{1,0:T(8,128)(2,1)}, bf16[512,2048]{1,0:T(8,128)(2,1)}) custom-call(s32[1]{0:T(128)} %bitcast.member_ref, s32[1]{0:T(128)} %bitcast.1.pair_ref, f32[512,512]{1,0:T(8,128)S(1)} %get-tuple-element.83.refs_3_.refs_0_, f32[512,512]{1,0:T(8,128)S(1)} %get-tuple-element.91.refs_1_, ...), custom_call_target="tpu_custom_call", output_to_operand_aliasing={{0}: (8, {}), {1}: (9, {})} | custom-call | flops 2000000000 | bytes 5000000 | tf_op jit(solution)/shard_map/pallas_call | solution.py:318
  112.4 1.8 %shard_map.132 = (bf16[512,2048]{1,0:T(8,128)(2,1)}, bf16[512,2048]{1,0:T(8,128)(2,1)}) custom-call(s32[1]{0:T(128)} %bitcast.member_ref, s32[1]{0:T(128)} %bitcast.1.pair_ref, f32[512,512]{1,0:T(8,128)S(1)} %get-tuple-element.88.refs_5_.refs_0_, f32[512,512]{1,0:T(8,128)S(1)} %get-tuple-element.89.refs_1_, ...), custom_call_target="tpu_custom_call", output_to_operand_aliasing={{0}: (8, {}), {1}: (9, {})} | custom-call | flops 2000000000 | bytes 5000000 | tf_op jit(solution)/shard_map/pallas_call | solution.py:318
  (71 shorter events, 24.7 us)
Async XLA Ops:
  0.6 1.6 %copy-start.2 = (bf16[512,2048]{1,0:T(8,128)(2,1)S(1)}, bf16[512,2048]{1,0:T(8,128)(2,1)}, u32[]{:S(2)}) copy-start(bf16[512,2048]{1,0:T(8,128)(2,1)} %refs_2_.31) | copy-start | bytes 6291460
  2.2 1.6 %copy-start.4 = (bf16[512,2048]{1,0:T(8,128)(2,1)S(1)}, bf16[512,2048]{1,0:T(8,128)(2,1)}, u32[]{:S(2)}) copy-start(bf16[512,2048]{1,0:T(8,128)(2,1)} %refs_3_.15) | copy-start | bytes 6291460
  3.8 0.8 copy-start.7
  5.7 10.3 %collective-permute-start.1 = (f32[520,128]{1,0:T(8,128)S(1)}, f32[520,128]{1,0:T(8,128)S(1)}, u32[]{:S(2)}, u32[]{:S(2)}) collective-permute-start(f32[520,128]{1,0:T(8,128)S(1)} %get-tuple-element.55.refs_3_), channel_id=1, source_target_pairs={{0,4},{4,0},{8,12},{12,8},{16,20},{20,16},{24,28},{28,24},{1,5},{5... | collective-permute-start | bytes 798728 | tf_op jit(solution)/shard_map/ppermute | solution.py:368
  9.5 11.3 %collective-permute-start = (f32[520,128]{1,0:T(8,128)S(1)}, f32[520,128]{1,0:T(8,128)S(1)}, u32[]{:S(2)}, u32[]{:S(2)}) collective-permute-start(f32[520,128]{1,0:T(8,128)S(1)} %shard_map.94.refs_3_), channel_id=1, source_target_pairs={{0,4},{4,0},{8,12},{12,8},{16,20},{20,16},{24,28},{28,24},{1,5},{5... | collective-permute-start | bytes 798728 | tf_op jit(solution)/shard_map/ppermute | solution.py:368
  10.4 1.6 %copy-start.1 = (bf16[512,2048]{1,0:T(8,128)(2,1)S(1)}, bf16[512,2048]{1,0:T(8,128)(2,1)}, u32[]{:S(2)}) copy-start(bf16[512,2048]{1,0:T(8,128)(2,1)} %refs_0_.23) | copy-start | bytes 6291460
  13.9 10.6 %copy-start.3 = (bf16[512,2048]{1,0:T(8,128)(2,1)S(1)}, bf16[512,2048]{1,0:T(8,128)(2,1)}, u32[]{:S(2)}) copy-start(bf16[512,2048]{1,0:T(8,128)(2,1)} %refs_2_.31) | copy-start | bytes 6291460
  16.0 10.5 %collective-permute-start.3 = (f32[512,128]{1,0:T(8,128)S(1)}, f32[512,128]{1,0:T(8,128)S(1)}, u32[]{:S(2)}, u32[]{:S(2)}) collective-permute-start(f32[512,128]{1,0:T(8,128)S(1)} %shard_map.98.refs_2_), channel_id=1, source_target_pairs={{0,8},{4,12},{1,9},{5,13},{2,10},{6,14},{3,11},{7,15}} | collective-permute-start | bytes 786440 | tf_op jit(solution)/shard_map/ppermute | solution.py:387
  20.9 8.6 %collective-permute-start.2 = (f32[512,128]{1,0:T(8,128)S(1)}, f32[512,128]{1,0:T(8,128)S(1)}, u32[]{:S(2)}, u32[]{:S(2)}) collective-permute-start(f32[512,128]{1,0:T(8,128)S(1)} %shard_map.99.refs_4_), channel_id=1, source_target_pairs={{0,8},{4,12},{1,9},{5,13},{2,10},{6,14},{3,11},{7,15}} | collective-permute-start | bytes 786440 | tf_op jit(solution)/shard_map/ppermute | solution.py:387
  26.5 3.7 %copy-start.5 = (bf16[512,2048]{1,0:T(8,128)(2,1)S(1)}, bf16[512,2048]{1,0:T(8,128)(2,1)}, u32[]{:S(2)}) copy-start(bf16[512,2048]{1,0:T(8,128)(2,1)} %refs_3_.15) | copy-start | bytes 6291460
  26.5 5.6 %collective-permute-start.5 = (f32[512,128]{1,0:T(8,128)S(1)}, f32[512,128]{1,0:T(8,128)S(1)}, u32[]{:S(2)}, u32[]{:S(2)}) collective-permute-start(f32[512,128]{1,0:T(8,128)S(1)} %shard_map.101.refs_3_), channel_id=1, source_target_pairs={{8,16},{12,20},{9,17},{13,21},{10,18},{14,22},{11,19},{15,23}} | collective-permute-start | bytes 786440 | tf_op jit(solution)/shard_map/ppermute | solution.py:387
  29.5 3.3 %collective-permute-start.4 = (f32[512,128]{1,0:T(8,128)S(1)}, f32[512,128]{1,0:T(8,128)S(1)}, u32[]{:S(2)}, u32[]{:S(2)}) collective-permute-start(f32[512,128]{1,0:T(8,128)S(1)} %shard_map.102.refs_4_), channel_id=1, source_target_pairs={{8,16},{12,20},{9,17},{13,21},{10,18},{14,22},{11,19},{15,23}} | collective-permute-start | bytes 786440 | tf_op jit(solution)/shard_map/ppermute | solution.py:387
  32.1 3.3 %collective-permute-start.7 = (f32[512,128]{1,0:T(8,128)S(1)}, f32[512,128]{1,0:T(8,128)S(1)}, u32[]{:S(2)}, u32[]{:S(2)}) collective-permute-start(f32[512,128]{1,0:T(8,128)S(1)} %shard_map.104.refs_3_), channel_id=1, source_target_pairs={{16,24},{20,28},{17,25},{21,29},{18,26},{22,30},{19,27},{23,31}} | collective-permute-start | bytes 786440 | tf_op jit(solution)/shard_map/ppermute | solution.py:387
  32.8 5.4 %collective-permute-start.6 = (f32[512,128]{1,0:T(8,128)S(1)}, f32[512,128]{1,0:T(8,128)S(1)}, u32[]{:S(2)}, u32[]{:S(2)}) collective-permute-start(f32[512,128]{1,0:T(8,128)S(1)} %shard_map.105.refs_4_), channel_id=1, source_target_pairs={{16,24},{20,28},{17,25},{21,29},{18,26},{22,30},{19,27},{23,31}} | collective-permute-start | bytes 786440 | tf_op jit(solution)/shard_map/ppermute | solution.py:387
  35.4 1.7 %copy-start = (bf16[512,2048]{1,0:T(8,128)(2,1)S(1)}, bf16[512,2048]{1,0:T(8,128)(2,1)}, u32[]{:S(2)}) copy-start(bf16[512,2048]{1,0:T(8,128)(2,1)} %refs_1_.35) | copy-start | bytes 6291460
  35.4 1.7 %copy-start.6 = (f32[2048]{0:T(1024)S(1)}, f32[2048]{0:T(1024)}, u32[]{:S(2)}) copy-start(f32[2048]{0:T(1024)} %param.10) | copy-start | bytes 24580
  35.5 9.3 %collective-permute-start.9 = (f32[512,128]{1,0:T(8,128)S(1)}, f32[512,128]{1,0:T(8,128)S(1)}, u32[]{:S(2)}, u32[]{:S(2)}) collective-permute-start(f32[512,128]{1,0:T(8,128)S(1)} %get-tuple-element.57.refs_7_), channel_id=1, source_target_pairs={{0,4},{4,0},{8,12},{12,8},{16,20},{20,16},{24,28},{28,24},{1,5},{5... | collective-permute-start | bytes 786440 | tf_op jit(solution)/shard_map/ppermute | solution.py:398
  38.3 9.4 %collective-permute-start.8 = (f32[512,128]{1,0:T(8,128)S(1)}, f32[512,128]{1,0:T(8,128)S(1)}, u32[]{:S(2)}, u32[]{:S(2)}) collective-permute-start(f32[512,128]{1,0:T(8,128)S(1)} %get-tuple-element.60.refs_7_), channel_id=1, source_target_pairs={{0,4},{4,0},{8,12},{12,8},{16,20},{20,16},{24,28},{28,24},{1,5},{5... | collective-permute-start | bytes 786440 | tf_op jit(solution)/shard_map/ppermute | solution.py:398
  48.8 1.7 %collective-permute-start.12 = (f32[8,512]{1,0:T(8,128)S(1)}, f32[8,512]{1,0:T(8,128)S(1)}, u32[]{:S(2)}, u32[]{:S(2)}) collective-permute-start(f32[8,512]{1,0:T(8,128)S(1)} %get-tuple-element.64.refs_5_), channel_id=1, source_target_pairs={{0,3},{1,0},{2,1},{3,2},{4,7},{5,4},{6,5},{7,6},{8,11},{9,8},{10,9... | collective-permute-start | bytes 49160 | tf_op jit(solution)/shard_map/ppermute | solution.py:461
  48.8 3.8 %collective-permute-start.11 = (f32[8,512]{1,0:T(8,128)S(1)}, f32[8,512]{1,0:T(8,128)S(1)}, u32[]{:S(2)}, u32[]{:S(2)}) collective-permute-start(f32[8,512]{1,0:T(8,128)S(1)} %get-tuple-element.64.refs_5_), channel_id=1, source_target_pairs={{0,2},{1,3},{2,0},{3,1},{4,6},{5,7},{6,4},{7,5},{8,10},{9,11},{10,... | collective-permute-start | bytes 49160 | tf_op jit(solution)/shard_map/ppermute | solution.py:461
  50.3 3.2 %collective-permute-start.10 = (f32[8,512]{1,0:T(8,128)S(1)}, f32[8,512]{1,0:T(8,128)S(1)}, u32[]{:S(2)}, u32[]{:S(2)}) collective-permute-start(f32[8,512]{1,0:T(8,128)S(1)} %get-tuple-element.64.refs_5_), channel_id=1, source_target_pairs={{0,1},{1,2},{2,3},{3,0},{4,5},{5,6},{6,7},{7,4},{8,9},{9,10},{10,1... | collective-permute-start | bytes 49160 | tf_op jit(solution)/shard_map/ppermute | solution.py:461
  55.2 9.3 %collective-permute-start.14 = (f32[520,128]{1,0:T(8,128)S(1)}, f32[520,128]{1,0:T(8,128)S(1)}, u32[]{:S(2)}, u32[]{:S(2)}) collective-permute-start(f32[520,128]{1,0:T(8,128)S(1)} %get-tuple-element.69.refs_10_), channel_id=1, source_target_pairs={{0,4},{4,0},{8,12},{12,8},{16,20},{20,16},{24,28},{28,24},{1,5},{5... | collective-permute-start | bytes 798728 | tf_op jit(solution)/shard_map/ppermute | solution.py:368
  58.5 9.3 %collective-permute-start.13 = (f32[520,128]{1,0:T(8,128)S(1)}, f32[520,128]{1,0:T(8,128)S(1)}, u32[]{:S(2)}, u32[]{:S(2)}) collective-permute-start(f32[520,128]{1,0:T(8,128)S(1)} %get-tuple-element.71.refs_10_), channel_id=1, source_target_pairs={{0,4},{4,0},{8,12},{12,8},{16,20},{20,16},{24,28},{28,24},{1,5},{5... | collective-permute-start | bytes 798728 | tf_op jit(solution)/shard_map/ppermute | solution.py:368
  64.6 7.8 %collective-permute-start.16 = (f32[512,128]{1,0:T(8,128)S(1)}, f32[512,128]{1,0:T(8,128)S(1)}, u32[]{:S(2)}, u32[]{:S(2)}) collective-permute-start(f32[512,128]{1,0:T(8,128)S(1)} %shard_map.117.refs_2_), channel_id=1, source_target_pairs={{24,16},{28,20},{25,17},{29,21},{26,18},{30,22},{27,19},{31,23}} | collective-permute-start | bytes 786440 | tf_op jit(solution)/shard_map/ppermute | solution.py:387
  67.8 5.3 %collective-permute-start.15 = (f32[512,128]{1,0:T(8,128)S(1)}, f32[512,128]{1,0:T(8,128)S(1)}, u32[]{:S(2)}, u32[]{:S(2)}) collective-permute-start(f32[512,128]{1,0:T(8,128)S(1)} %shard_map.118.refs_6_), channel_id=1, source_target_pairs={{24,16},{28,20},{25,17},{29,21},{26,18},{30,22},{27,19},{31,23}} | collective-permute-start | bytes 786440 | tf_op jit(solution)/shard_map/ppermute | solution.py:387
  72.4 5.4 %collective-permute-start.18 = (f32[512,128]{1,0:T(8,128)S(1)}, f32[512,128]{1,0:T(8,128)S(1)}, u32[]{:S(2)}, u32[]{:S(2)}) collective-permute-start(f32[512,128]{1,0:T(8,128)S(1)} %shard_map.120.refs_3_), channel_id=1, source_target_pairs={{16,8},{20,12},{17,9},{21,13},{18,10},{22,14},{19,11},{23,15}} | collective-permute-start | bytes 786440 | tf_op jit(solution)/shard_map/ppermute | solution.py:387
  73.1 5.9 %collective-permute-start.17 = (f32[512,128]{1,0:T(8,128)S(1)}, f32[512,128]{1,0:T(8,128)S(1)}, u32[]{:S(2)}, u32[]{:S(2)}) collective-permute-start(f32[512,128]{1,0:T(8,128)S(1)} %shard_map.121.refs_7_), channel_id=1, source_target_pairs={{16,8},{20,12},{17,9},{21,13},{18,10},{22,14},{19,11},{23,15}} | collective-permute-start | bytes 786440 | tf_op jit(solution)/shard_map/ppermute | solution.py:387
  77.7 22.6 %collective-permute-start.19 = (f32[512,128]{1,0:T(8,128)S(1)}, f32[512,128]{1,0:T(8,128)S(1)}, u32[]{:S(2)}, u32[]{:S(2)}) collective-permute-start(f32[512,128]{1,0:T(8,128)S(1)} %shard_map.123.refs_3_), channel_id=1, source_target_pairs={{8,0},{12,4},{9,1},{13,5},{10,2},{14,6},{11,3},{15,7}} | collective-permute-start | bytes 786440 | tf_op jit(solution)/shard_map/ppermute | solution.py:387
  79.0 26.8 %collective-permute-start.20 = (f32[512,128]{1,0:T(8,128)S(1)}, f32[512,128]{1,0:T(8,128)S(1)}, u32[]{:S(2)}, u32[]{:S(2)}) collective-permute-start(f32[512,128]{1,0:T(8,128)S(1)} %shard_map.124.refs_7_), channel_id=1, source_target_pairs={{8,0},{12,4},{9,1},{13,5},{10,2},{14,6},{11,3},{15,7}} | collective-permute-start | bytes 786440 | tf_op jit(solution)/shard_map/ppermute | solution.py:387
  100.4 9.7 %collective-permute-start.22 = (f32[512,128]{1,0:T(8,128)S(1)}, f32[512,128]{1,0:T(8,128)S(1)}, u32[]{:S(2)}, u32[]{:S(2)}) collective-permute-start(f32[512,128]{1,0:T(8,128)S(1)} %get-tuple-element.86.refs_7_), channel_id=1, source_target_pairs={{0,4},{4,0},{8,12},{12,8},{16,20},{20,16},{24,28},{28,24},{1,5},{5... | collective-permute-start | bytes 786440 | tf_op jit(solution)/shard_map/ppermute | solution.py:398
  105.9 6.4 %collective-permute-start.21 = (f32[512,128]{1,0:T(8,128)S(1)}, f32[512,128]{1,0:T(8,128)S(1)}, u32[]{:S(2)}, u32[]{:S(2)}) collective-permute-start(f32[512,128]{1,0:T(8,128)S(1)} %get-tuple-element.90.refs_6_), channel_id=1, source_target_pairs={{0,4},{4,0},{8,12},{12,8},{16,20},{20,16},{24,28},{28,24},{1,5},{5... | collective-permute-start | bytes 786440 | tf_op jit(solution)/shard_map/ppermute | solution.py:398
where the time goes:
time: 115 us; the launch traced here: 114 us
  Pallas kernels  45.6 us (40%)
  waiting for transfers between devices  35 us (30%)
  starting transfers between devices  27.8 us (24%)
  local copies, waits for them, and re-layouts  4.73 us (4%)
    pallas_call x40, Pallas kernels, run(): pl.pallas_call(body, out_shape=[shape for shape, _ in outs], grid_spec=pl...  45.6 us
    ppermute x12, waiting for transfers between devices, chain(): arrived[c, p + 1] = lax.ppermute(value, 'seq', pairs)  18.2 us
    ppermute x12, starting transfers between devices, chain(): arrived[c, p + 1] = lax.ppermute(value, 'seq', pairs)  15.7 us
    ppermute x4, waiting for transfers between devices, chain(): received.append(lax.ppermute(sent, 'seq', swap))  7.56 us
    ppermute x4, waiting for transfers between devices, chain(): theirs.append(lax.ppermute(send, 'seq', swap))  6.28 us
    ppermute x4, starting transfers between devices, chain(): theirs.append(lax.ppermute(send, 'seq', swap))  5.2 us
    ppermute x4, starting transfers between devices, chain(): received.append(lax.ppermute(sent, 'seq', swap))  5.15 us
    unnamed x16, local copies, waits for them, and re-layouts  4.73 us
  transfers between devices with their start and end apart: 23, of which 11 were waited for; matrix products, arithmetic and copies ran while one was open for 0% of the time, Pallas kernels for 35%

commit v1 on v0

--- a/solution.py
+++ b/solution.py
@@ -107,7 +107,12 @@
     def _():
         cumul_ref[...] = cumulative(decay_ref[...])
 
-    pieces_kernel(part, info, key_ref, value_ref, cumul_ref, out_ref)
+    for j in range(part.per_step):
+        row = part.row(cumul_ref, info, j)
+        out_ref[part.state_rows(j), :] = outer_sum(
+            key_ref[:, cols(j)], trail_row(row), value_ref[:, cols(j)]
+        )
+    store_decays(part, info, cumul_ref, out_ref)
 
 
 def inner_kernel(part, info, query_ref, key_ref, value_ref, cumul_ref, out_ref):
@@ -255,6 +260,10 @@
     return member == 1, places - 1 - pair
 
 
+def copy_kernel(info, in_ref, out_ref):
+    out_ref[...] = in_ref[...]
+
+
 def hop_kernel(half, p, position, info, keep_ref, got_ref, *refs):
     arrived, out_ref = refs[:-1], refs[-1]
     is_first, place = position(info)
@@ -308,7 +317,7 @@
     sums_shape = jax.ShapeDtypeStruct((8, tokens), f32)
     info = (member.astype(jnp.int32).reshape(1), pair.astype(jnp.int32).reshape(1))
 
-    def run(kernel, grid, ins, outs, scratch=(), after=(), aliases=None, cost=1.0):
+    def run(kernel, grid, ins, outs, scratch=(), after=(), aliases=None, cost=1.0, limit=24):
         used = len(ins)
         after = [x for i, x in enumerate(after) if not any(x is y for y in after[:i])]
 
@@ -326,7 +335,7 @@
                 scratch_shapes=list(scratch),
             ),
             input_output_aliases=aliases or {},
-            compiler_params=pltpu.CompilerParams(vmem_limit_bytes=24 * 1024 * 1024),
+            compiler_params=pltpu.CompilerParams(vmem_limit_bytes=limit * 1024 * 1024),
             cost_estimate=pl.CostEstimate(
                 flops=int(cost * 1e9), bytes_accessed=int(cost * 2.5e6), transcendentals=0
             ),
@@ -362,18 +371,19 @@
         def device(place, m):
             return 2 * (place if forward else places - 1 - place) + m
 
-        received, last = [], ()
-        for c in range(CHUNKS):
-            sent = make_piece(their_parts[c], last)
+        sends, keeps, last = [], [], ()
+        for part in their_parts + mine_parts:
+            piece = make_piece(part, last)
+            (sends if part.slot == "theirs" else keeps).append(piece)
+            last = () if forward and len(sends) == 1 else (piece,)
+        for work in early:
+            last = (work(last),)
+        received = [lax.ppermute(sends[0], "seq", swap)]
+        for c in range(1, CHUNKS):
+            sent, = run(copy_kernel, 1, [plain(sends[c])], [give(wide_state)], after=last, cost=0.2)
             received.append(lax.ppermute(sent, "seq", swap))
             last = (sent,)
-        keeps = []
-        for c in range(CHUNKS):
-            keeps.append(make_piece(mine_parts[c], last))
-            last = (keeps[-1],)
-        for work in early:
-            last = (work(last),)
-        arrived, mine, theirs = {}, [], []
+        arrived, mine, theirs, done = {}, [], [], []
         for p in range(places - 1):
             pairs = [(device(p, m), device(p + 1, m)) for m in (0, 1)]
             for c in range(CHUNKS):
@@ -386,8 +396,9 @@
                 )
                 arrived[c, p + 1] = lax.ppermute(value, "seq", pairs)
                 last = (value,)
-            if filler:
-                last = (filler.pop(0)(last),)
+            for _ in range(-(-len(filler) // (places - 1 - p)) if p else 1):
+                if filler:
+                    last = (filler.pop(0)(last),)
         for c in range(CHUNKS):
             ins = [plain(keeps[c]), plain(received[c])]
             ins += [plain(arrived[c, p]) for p in range(1, places)]
@@ -398,7 +409,10 @@
             theirs.append(lax.ppermute(send, "seq", swap))
             mine.append(own)
             last = (send,)
-            filler.append(functools.partial(on_mine, c, own))
+            if c < CHUNKS - 1 and not forward:
+                continue
+            filler += [functools.partial(on_mine, i, mine[i]) for i in range(len(mine)) if i not in done]
+            done += range(len(mine))
             last = (filler.pop(0)(last),)
         while filler:
             last = (filler.pop(0)(last),)
@@ -410,8 +424,9 @@
         if not held_cumul:
             piece, cumul = part.call(
                 first_pieces_kernel,
-                [plain(key_vecs), plain(value_vecs), plain(log_decay.T)],
+                [(key_vecs, part.full_spec()), (value_vecs, part.full_spec()), plain(log_decay.T)],
                 [give(wide_state), give(jax.ShapeDtypeStruct((heads, tokens), f32))], cost=1.0,
+                limit=60,
             )
             held_cumul.append(cumul)
             return piece

time: 115 us -> 114 us (level)
  starting transfers between devices: 27.8 us -> 23.8 us
  waiting for transfers between devices: 35 us -> 37.2 us
  Pallas kernels: 45.6 us -> 47.6 us
    ppermute x4, starting transfers between devices: 5.2 us -> 1.46 us  [chain(): theirs.append(lax.ppermute(send, 'seq', swap))]
    ppermute x4 -> x2, starting transfers between devices: 5.15 us -> 1.67 us  [chain(): received.append(lax.ppermute(sent, 'seq', swap))]
    ppermute x0 -> x2, starting transfers between devices: none -> 3.48 us  [chain(): received = [lax.ppermute(sends[0], 'seq', swap)]]
    ppermute x4, waiting for transfers between devices: 6.28 us -> 9 us  [chain(): theirs.append(lax.ppermute(send, 'seq', swap))]
    pallas_call x40 -> x42, Pallas kernels: 45.6 us -> 47.6 us  [run(): pl.pallas_call(body, out_shape=[shape for shape, _ in outs], grid_spec=pl...]
    ppermute x12, waiting for transfers between devices: 18.2 us -> 16.9 us  [chain(): arrived[c, p + 1] = lax.ppermute(value, 'seq', pairs)]
    ppermute x4 -> x2, waiting for transfers between devices: 7.56 us -> 8.31 us  [chain(): received.append(lax.ppermute(sent, 'seq', swap))]
where the time goes in v1:
time: 114 us
  Pallas kernels  47.6 us (42%)
  waiting for transfers between devices  37.2 us (33%)
  starting transfers between devices  23.8 us (21%)
  local copies, waits for them, and re-layouts  4.04 us (4%)
    pallas_call x42, Pallas kernels, run(): pl.pallas_call(body, out_shape=[shape for shape, _ in outs], grid_spec=pl...  47.6 us
    ppermute x12, waiting for transfers between devices, chain(): arrived[c, p + 1] = lax.ppermute(value, 'seq', pairs)  16.9 us
    ppermute x12, starting transfers between devices, chain(): arrived[c, p + 1] = lax.ppermute(value, 'seq', pairs)  15.4 us
    ppermute x4, waiting for transfers between devices, chain(): theirs.append(lax.ppermute(send, 'seq', swap))  9 us
    ppermute x2, waiting for transfers between devices, chain(): received.append(lax.ppermute(sent, 'seq', swap))  8.31 us
    unnamed x16, local copies, waits for them, and re-layouts  4.03 us
    ppermute x2, starting transfers between devices, chain(): received = [lax.ppermute(sends[0], 'seq', swap)]  3.48 us
    ppermute x3, waiting for transfers between devices, on_device(): lax.ppermute(sums, 'head', [(i, (i + k) % head_count) for i in range(head...  2.96 us
  transfers between devices with their start and end apart: 23, of which 11 were waited for; matrix products, arithmetic and copies ran while one was open for 0% of the time, Pallas kernels for 35%

profile of v1, /device:TPU:0, one launch (start us, length us, event | category | flops | bytes accessed | tf_op | source)
XLA Modules:
  0.0 113.6 jit_solution(3682099259565996304)
XLA Ops:
  0.7 3.0 %shard_map.93 = (f32[520,128]{1,0:T(8,128)}, f32[16,512]{1,0:T(8,128)}) custom-call(s32[1]{0:T(128)} %bitcast.member_ref, s32[1]{0:T(128)} %bitcast.1.pair_ref, bf16[512,2048]{1,0:T(8,128)(2,1)} %refs_2_.31, bf16[512,2048]{1,0:T(8,128)(2,1)} %refs_3_.15, f32[16,512]{1,0:T(8,128)} %bitcast.12), custom_call_target="tpu_custom_call" | custom-call | flops 1000000000 | bytes 2500000 | tf_op jit(solution)/shard_map/pallas_call | solution.py:327
  3.6 3.0 %collective-permute-start.1 = (f32[520,128]{1,0:T(8,128)}, f32[520,128]{1,0:T(8,128)S(1)}, u32[]{:S(2)}, u32[]{:S(2)}) collective-permute-start(f32[520,128]{1,0:T(8,128)} %get-tuple-element.55), channel_id=1, source_target_pairs={{0,4},{4,0},{8,12},{12,8},{16,20},{20,16},{24,28},{28,24},{1,5},{5... | collective-permute-start | bytes 798728 | tf_op jit(solution)/shard_map/ppermute | solution.py:381
  6.6 1.6 %copy-done.3 = bf16[512,2048]{1,0:T(8,128)(2,1)S(1)} copy-done((bf16[512,2048]{1,0:T(8,128)(2,1)S(1)}, bf16[512,2048]{1,0:T(8,128)(2,1)}, u32[]{:S(2)}) %copy-start.3) | copy-done | bytes 2097176
  12.1 1.9 %shard_map.97.refs_1_.refs_0_ = f32[512,512]{1,0:T(8,128)S(1)} custom-call(s32[1]{0:T(128)} %bitcast.member_ref, s32[1]{0:T(128)} %bitcast.1.pair_ref, bf16[512,2048]{1,0:T(8,128)(2,1)S(1)} %copy-done.1, bf16[512,2048]{1,0:T(8,128)(2,1)S(1)} %copy-done.2, bf16[512,2048]{1,0:T(8,128)(2,1)S(1)} %copy-done.3, f32[16,512]{1,0:T(8,128)S(1)} %copy-done.5, ...), custom_call_target="tpu_custom_call" | custom-call | flops 2200000000 | bytes 5500000 | tf_op jit(solution)/shard_map/pallas_call | solution.py:327
  14.2 4.0 %collective-permute-start.3 = (f32[512,128]{1,0:T(8,128)S(1)}, f32[512,128]{1,0:T(8,128)S(1)}, u32[]{:S(2)}, u32[]{:S(2)}) collective-permute-start(f32[512,128]{1,0:T(8,128)S(1)} %shard_map.99.refs_2_), channel_id=1, source_target_pairs={{0,8},{4,12},{1,9},{5,13},{2,10},{6,14},{3,11},{7,15}} | collective-permute-start | bytes 786440 | tf_op jit(solution)/shard_map/ppermute | solution.py:397
  18.3 3.7 %collective-permute-done.refs_1_ = f32[520,128]{1,0:T(8,128)S(1)} collective-permute-done((f32[520,128]{1,0:T(8,128)S(1)}, f32[520,128]{1,0:T(8,128)S(1)}, u32[]{:S(2)}, u32[]{:S(2)}) %collective-permute-start) | collective-permute-done | bytes 266272 | tf_op jit(solution)/shard_map/ppermute | solution.py:384
  22.1 3.4 %collective-permute-start.2 = (f32[512,128]{1,0:T(8,128)S(1)}, f32[512,128]{1,0:T(8,128)S(1)}, u32[]{:S(2)}, u32[]{:S(2)}) collective-permute-start(f32[512,128]{1,0:T(8,128)S(1)} %shard_map.100.refs_4_), channel_id=1, source_target_pairs={{0,8},{4,12},{1,9},{5,13},{2,10},{6,14},{3,11},{7,15}} | collective-permute-start | bytes 786440 | tf_op jit(solution)/shard_map/ppermute | solution.py:397
  25.5 1.9 %shard_map.101.refs_3_.refs_0_ = f32[512,512]{1,0:T(8,128)S(1)} custom-call(s32[1]{0:T(128)} %bitcast.member_ref, s32[1]{0:T(128)} %bitcast.1.pair_ref, bf16[512,2048]{1,0:T(8,128)(2,1)S(1)} %copy-done.1, bf16[512,2048]{1,0:T(8,128)(2,1)S(1)} %copy-done.2, bf16[512,2048]{1,0:T(8,128)(2,1)S(1)} %copy-done.4, f32[16,512]{1,0:T(8,128)S(1)} %copy-done.5, ...), custom_call_target="tpu_custom_call" | custom-call | flops 2200000000 | bytes 5500000 | tf_op jit(solution)/shard_map/pallas_call | solution.py:327
  28.1 1.7 %collective-permute-done.2.refs_2_ = f32[512,128]{1,0:T(8,128)S(1)} collective-permute-done((f32[512,128]{1,0:T(8,128)S(1)}, f32[512,128]{1,0:T(8,128)S(1)}, u32[]{:S(2)}, u32[]{:S(2)}) %collective-permute-start.2) | collective-permute-done | bytes 262176 | tf_op jit(solution)/shard_map/ppermute | solution.py:397
  30.5 1.9 %shard_map.104.refs_3_.refs_0_ = f32[512,512]{1,0:T(8,128)S(1)} custom-call(s32[1]{0:T(128)} %bitcast.member_ref, s32[1]{0:T(128)} %bitcast.1.pair_ref, bf16[512,2048]{1,0:T(8,128)(2,1)S(1)} %copy-done.1, bf16[512,2048]{1,0:T(8,128)(2,1)S(1)} %copy-done.2, bf16[512,2048]{1,0:T(8,128)(2,1)S(1)} %copy-done.4, f32[16,512]{1,0:T(8,128)S(1)} %copy-done.6, ...), custom_call_target="tpu_custom_call" | custom-call | flops 2200000000 | bytes 5500000 | tf_op jit(solution)/shard_map/pallas_call | solution.py:327
  33.9 1.9 %shard_map.107.refs_5_.refs_0_ = f32[512,512]{1,0:T(8,128)S(1)} custom-call(s32[1]{0:T(128)} %bitcast.member_ref, s32[1]{0:T(128)} %bitcast.1.pair_ref, bf16[512,2048]{1,0:T(8,128)(2,1)S(1)} %copy-done.1, bf16[512,2048]{1,0:T(8,128)(2,1)S(1)} %copy-done.2, bf16[512,2048]{1,0:T(8,128)(2,1)S(1)} %copy-done.4, f32[16,512]{1,0:T(8,128)S(1)} %copy-done.6, ...), custom_call_target="tpu_custom_call" | custom-call | flops 2200000000 | bytes 5500000 | tf_op jit(solution)/shard_map/pallas_call | solution.py:327
  40.5 4.3 %collective-permute-done.9.refs_5_ = f32[512,128]{1,0:T(8,128)S(1)} collective-permute-done((f32[512,128]{1,0:T(8,128)S(1)}, f32[512,128]{1,0:T(8,128)S(1)}, u32[]{:S(2)}, u32[]{:S(2)}) %collective-permute-start.9) | collective-permute-done | bytes 262176 | tf_op jit(solution)/shard_map/ppermute | solution.py:409
  45.8 1.7 %collective-permute-done.8.refs_5_ = f32[512,128]{1,0:T(8,128)S(1)} collective-permute-done((f32[512,128]{1,0:T(8,128)S(1)}, f32[512,128]{1,0:T(8,128)S(1)}, u32[]{:S(2)}, u32[]{:S(2)}) %collective-permute-start.8) | collective-permute-done | bytes 262176 | tf_op jit(solution)/shard_map/ppermute | solution.py:409
  48.6 1.5 %collective-permute-start.11 = (f32[8,512]{1,0:T(8,128)S(1)}, f32[8,512]{1,0:T(8,128)S(1)}, u32[]{:S(2)}, u32[]{:S(2)}) collective-permute-start(f32[8,512]{1,0:T(8,128)S(1)} %get-tuple-element.64.refs_5_), channel_id=1, source_target_pairs={{0,2},{1,3},{2,0},{3,1},{4,6},{5,7},{6,4},{7,5},{8,10},{9,11},{10,... | collective-permute-start | bytes 49160 | tf_op jit(solution)/shard_map/ppermute | solution.py:476
  50.4 2.1 %collective-permute-done.11.refs_7_ = f32[8,512]{1,0:T(8,128)S(1)} collective-permute-done((f32[8,512]{1,0:T(8,128)S(1)}, f32[8,512]{1,0:T(8,128)S(1)}, u32[]{:S(2)}, u32[]{:S(2)}) %collective-permute-start.11) | collective-permute-done | bytes 16416 | tf_op jit(solution)/shard_map/ppermute | solution.py:476
  53.3 1.7 %shard_map.114 = (bf16[512,2048]{1,0:T(8,128)(2,1)}, bf16[512,512]{1,0:T(8,128)(2,1)S(1)}, f32[520,128]{1,0:T(8,128)S(1)}) custom-call(s32[1]{0:T(128)} %bitcast.member_ref, s32[1]{0:T(128)} %bitcast.1.pair_ref, f32[512,512]{1,0:T(8,128)S(1)} %get-tuple-element.67.refs_0_, bf16[512,2048]{1,0:T(8,128)(2,1)S(1)} %copy-done, f32[1,2048]{1,0:T(1,128)S(1)} %bitcast.8, ...), custom_call_target="tpu_custom_call" | custom-call | flops 2000000000 | bytes 5000000 | tf_op jit(solution)/shard_map/pallas_call | solution.py:327
  55.6 1.7 %shard_map.115 = (bf16[512,2048]{1,0:T(8,128)(2,1)}, bf16[512,512]{1,0:T(8,128)(2,1)S(1)}, f32[520,128]{1,0:T(8,128)S(1)}) custom-call(s32[1]{0:T(128)} %bitcast.member_ref, s32[1]{0:T(128)} %bitcast.1.pair_ref, f32[512,512]{1,0:T(8,128)S(1)} %get-tuple-element.66.refs_0_, bf16[512,2048]{1,0:T(8,128)(2,1)S(1)} %copy-done, ...), custom_call_target="tpu_custom_call", output_to_operand_aliasing={{0}: (11, {})} | custom-call | flops 2000000000 | bytes 5000000 | tf_op jit(solution)/shard_map/pallas_call | solution.py:327
  57.3 1.7 %shard_map.116 = (bf16[512,2048]{1,0:T(8,128)(2,1)}, bf16[512,512]{1,0:T(8,128)(2,1)S(1)}, f32[520,128]{1,0:T(8,128)S(1)}) custom-call(s32[1]{0:T(128)} %bitcast.member_ref, s32[1]{0:T(128)} %bitcast.1.pair_ref, f32[512,512]{1,0:T(8,128)S(1)} %get-tuple-element.65.refs_0_, bf16[512,2048]{1,0:T(8,128)(2,1)S(1)} %copy-done, ...), custom_call_target="tpu_custom_call", output_to_operand_aliasing={{0}: (11, {})} | custom-call | flops 2000000000 | bytes 5000000 | tf_op jit(solution)/shard_map/pallas_call | solution.py:327
  59.0 1.7 %shard_map.117 = (bf16[512,2048]{1,0:T(8,128)(2,1)}, bf16[512,512]{1,0:T(8,128)(2,1)S(1)}, f32[520,128]{1,0:T(8,128)S(1)}) custom-call(s32[1]{0:T(128)} %bitcast.member_ref, s32[1]{0:T(128)} %bitcast.1.pair_ref, f32[512,512]{1,0:T(8,128)S(1)} %get-tuple-element.61.refs_0_, bf16[512,2048]{1,0:T(8,128)(2,1)S(1)} %copy-done, ...), custom_call_target="tpu_custom_call", output_to_operand_aliasing={{0}: (11, {})} | custom-call | flops 2000000000 | bytes 5000000 | tf_op jit(solution)/shard_map/pallas_call | solution.py:327
  60.7 1.6 %collective-permute-start.13 = (f32[520,128]{1,0:T(8,128)S(1)}, f32[520,128]{1,0:T(8,128)S(1)}, u32[]{:S(2)}, u32[]{:S(2)}) collective-permute-start(f32[520,128]{1,0:T(8,128)S(1)} %shard_map.118.refs_2_), channel_id=1, source_target_pairs={{0,4},{4,0},{8,12},{12,8},{16,20},{20,16},{24,28},{28,24},{1,5},{5... | collective-permute-start | bytes 798728 | tf_op jit(solution)/shard_map/ppermute | solution.py:384
  63.0 4.6 %collective-permute-done.13.refs_1_ = f32[520,128]{1,0:T(8,128)S(1)} collective-permute-done((f32[520,128]{1,0:T(8,128)S(1)}, f32[520,128]{1,0:T(8,128)S(1)}, u32[]{:S(2)}, u32[]{:S(2)}) %collective-permute-start.13) | collective-permute-done | bytes 266272 | tf_op jit(solution)/shard_map/ppermute | solution.py:384
  68.3 3.9 %shard_map.121 = (bf16[512,2048]{1,0:T(8,128)(2,1)}, f32[512,512]{1,0:T(8,128)S(1)}, f32[512,512]{1,0:T(8,128)S(1)}) custom-call(s32[1]{0:T(128)} %bitcast.member_ref, s32[1]{0:T(128)} %bitcast.1.pair_ref, bf16[512,2048]{1,0:T(8,128)(2,1)S(1)} %copy-done.1, bf16[512,2048]{1,0:T(8,128)(2,1)S(1)} %copy-done.2, bf16[512,2048]{1,0:T(8,128)(2,1)S(1)} %copy-done.4, ...), custom_call_target="tpu_custom_call" | custom-call | flops 4300000256 | bytes 10750000 | tf_op jit(solution)/shard_map/pallas_call | solution.py:327
  73.6 4.0 %shard_map.124 = (bf16[512,2048]{1,0:T(8,128)(2,1)}, f32[512,512]{1,0:T(8,128)S(1)}, f32[512,512]{1,0:T(8,128)S(1)}) custom-call(s32[1]{0:T(128)} %bitcast.member_ref, s32[1]{0:T(128)} %bitcast.1.pair_ref, bf16[512,2048]{1,0:T(8,128)(2,1)S(1)} %copy-done.1, bf16[512,2048]{1,0:T(8,128)(2,1)S(1)} %copy-done.2, ...), custom_call_target="tpu_custom_call", output_to_operand_aliasing={{0}: (8, {})} | custom-call | flops 4300000256 | bytes 10750000 | tf_op jit(solution)/shard_map/pallas_call | solution.py:327
  77.6 3.9 %shard_map.125 = (bf16[512,2048]{1,0:T(8,128)(2,1)}, f32[512,512]{1,0:T(8,128)S(1)}, f32[512,512]{1,0:T(8,128)S(1)}) custom-call(s32[1]{0:T(128)} %bitcast.member_ref, s32[1]{0:T(128)} %bitcast.1.pair_ref, bf16[512,2048]{1,0:T(8,128)(2,1)S(1)} %copy-done.1, bf16[512,2048]{1,0:T(8,128)(2,1)S(1)} %copy-done.2, ...), custom_call_target="tpu_custom_call", output_to_operand_aliasing={{0}: (8, {})} | custom-call | flops 4300000256 | bytes 10750000 | tf_op jit(solution)/shard_map/pallas_call | solution.py:327
  84.1 4.0 %shard_map.128 = (bf16[512,2048]{1,0:T(8,128)(2,1)}, f32[512,512]{1,0:T(8,128)S(1)}, f32[512,512]{1,0:T(8,128)S(1)}) custom-call(s32[1]{0:T(128)} %bitcast.member_ref, s32[1]{0:T(128)} %bitcast.1.pair_ref, bf16[512,2048]{1,0:T(8,128)(2,1)S(1)} %copy-done.1, bf16[512,2048]{1,0:T(8,128)(2,1)S(1)} %copy-done.2, ...), custom_call_target="tpu_custom_call", output_to_operand_aliasing={{0}: (8, {})} | custom-call | flops 4300000256 | bytes 10750000 | tf_op jit(solution)/shard_map/pallas_call | solution.py:327
  88.1 12.5 %collective-permute-done.20.refs_4_ = f32[512,128]{1,0:T(8,128)S(1)} collective-permute-done((f32[512,128]{1,0:T(8,128)S(1)}, f32[512,128]{1,0:T(8,128)S(1)}, u32[]{:S(2)}, u32[]{:S(2)}) %collective-permute-start.20) | collective-permute-done | bytes 262176 | tf_op jit(solution)/shard_map/ppermute | solution.py:397
  100.7 2.7 %collective-permute-done.19.refs_4_ = f32[512,128]{1,0:T(8,128)S(1)} collective-permute-done((f32[512,128]{1,0:T(8,128)S(1)}, f32[512,128]{1,0:T(8,128)S(1)}, u32[]{:S(2)}, u32[]{:S(2)}) %collective-permute-start.19) | collective-permute-done | bytes 262176 | tf_op jit(solution)/shard_map/ppermute | solution.py:397
  103.5 1.8 %shard_map.131 = (bf16[512,2048]{1,0:T(8,128)(2,1)}, bf16[512,2048]{1,0:T(8,128)(2,1)}) custom-call(s32[1]{0:T(128)} %bitcast.member_ref, s32[1]{0:T(128)} %bitcast.1.pair_ref, f32[512,512]{1,0:T(8,128)S(1)} %get-tuple-element.81.refs_3_.refs_0_, f32[512,512]{1,0:T(8,128)S(1)} %get-tuple-element.94.refs_1_, bf16[512,2048]{1,0:T(8,128)(2,1)S(1)} %copy-done.2, ...), custom_call_target="tpu_custom_call" | custom-call | flops 2000000000 | bytes 5000000 | tf_op jit(solution)/shard_map/pallas_call | solution.py:327
  105.3 1.7 %shard_map.132 = (bf16[512,2048]{1,0:T(8,128)(2,1)}, bf16[512,2048]{1,0:T(8,128)(2,1)}) custom-call(s32[1]{0:T(128)} %bitcast.member_ref, s32[1]{0:T(128)} %bitcast.1.pair_ref, f32[512,512]{1,0:T(8,128)S(1)} %get-tuple-element.85.refs_3_.refs_0_, f32[512,512]{1,0:T(8,128)S(1)} %get-tuple-element.92.refs_1_, ...), custom_call_target="tpu_custom_call", output_to_operand_aliasing={{0}: (8, {}), {1}: (9, {})} | custom-call | flops 2000000000 | bytes 5000000 | tf_op jit(solution)/shard_map/pallas_call | solution.py:327
  107.1 2.0 %collective-permute-done.22.refs_5_ = f32[512,128]{1,0:T(8,128)S(1)} collective-permute-done((f32[512,128]{1,0:T(8,128)S(1)}, f32[512,128]{1,0:T(8,128)S(1)}, u32[]{:S(2)}, u32[]{:S(2)}) %collective-permute-start.22) | collective-permute-done | bytes 262176 | tf_op jit(solution)/shard_map/ppermute | solution.py:409
  109.1 1.8 %shard_map.133 = (bf16[512,2048]{1,0:T(8,128)(2,1)}, bf16[512,2048]{1,0:T(8,128)(2,1)}) custom-call(s32[1]{0:T(128)} %bitcast.member_ref, s32[1]{0:T(128)} %bitcast.1.pair_ref, f32[512,512]{1,0:T(8,128)S(1)} %get-tuple-element.83.refs_7_.refs_0_, f32[512,512]{1,0:T(8,128)S(1)} %get-tuple-element.91.refs_1_, ...), custom_call_target="tpu_custom_call", output_to_operand_aliasing={{0}: (8, {}), {1}: (9, {})} | custom-call | flops 2000000000 | bytes 5000000 | tf_op jit(solution)/shard_map/pallas_call | solution.py:327
  111.9 1.8 %shard_map.134 = (bf16[512,2048]{1,0:T(8,128)(2,1)}, bf16[512,2048]{1,0:T(8,128)(2,1)}) custom-call(s32[1]{0:T(128)} %bitcast.member_ref, s32[1]{0:T(128)} %bitcast.1.pair_ref, f32[512,512]{1,0:T(8,128)S(1)} %get-tuple-element.87.refs_5_.refs_0_, f32[512,512]{1,0:T(8,128)S(1)} %get-tuple-element.88.refs_1_, ...), custom_call_target="tpu_custom_call", output_to_operand_aliasing={{0}: (8, {}), {1}: (9, {})} | custom-call | flops 2000000000 | bytes 5000000 | tf_op jit(solution)/shard_map/pallas_call | solution.py:327
  (73 shorter events, 22.0 us)
Async XLA Ops:
  0.7 5.9 %copy-start.2 = (bf16[512,2048]{1,0:T(8,128)(2,1)S(1)}, bf16[512,2048]{1,0:T(8,128)(2,1)}, u32[]{:S(2)}) copy-start(bf16[512,2048]{1,0:T(8,128)(2,1)} %refs_2_.31) | copy-start | bytes 6291460
  3.6 10.6 %collective-permute-start.1 = (f32[520,128]{1,0:T(8,128)}, f32[520,128]{1,0:T(8,128)S(1)}, u32[]{:S(2)}, u32[]{:S(2)}) collective-permute-start(f32[520,128]{1,0:T(8,128)} %get-tuple-element.55), channel_id=1, source_target_pairs={{0,4},{4,0},{8,12},{12,8},{16,20},{20,16},{24,28},{28,24},{1,5},{5... | collective-permute-start | bytes 798728 | tf_op jit(solution)/shard_map/ppermute | solution.py:381
  6.6 1.6 %copy-start.3 = (bf16[512,2048]{1,0:T(8,128)(2,1)S(1)}, bf16[512,2048]{1,0:T(8,128)(2,1)}, u32[]{:S(2)}) copy-start(bf16[512,2048]{1,0:T(8,128)(2,1)} %refs_3_.15) | copy-start | bytes 6291460
  8.2 0.8 copy-start.5
  10.5 1.6 %copy-start.1 = (bf16[512,2048]{1,0:T(8,128)(2,1)S(1)}, bf16[512,2048]{1,0:T(8,128)(2,1)}, u32[]{:S(2)}) copy-start(bf16[512,2048]{1,0:T(8,128)(2,1)} %refs_0_.23) | copy-start | bytes 6291460
  14.0 11.5 %copy-start.4 = (bf16[512,2048]{1,0:T(8,128)(2,1)S(1)}, bf16[512,2048]{1,0:T(8,128)(2,1)}, u32[]{:S(2)}) copy-start(bf16[512,2048]{1,0:T(8,128)(2,1)} %refs_3_.15) | copy-start | bytes 6291460
  14.1 7.9 %collective-permute-start = (f32[520,128]{1,0:T(8,128)S(1)}, f32[520,128]{1,0:T(8,128)S(1)}, u32[]{:S(2)}, u32[]{:S(2)}) collective-permute-start(f32[520,128]{1,0:T(8,128)S(1)} %shard_map.98.refs_2_), channel_id=1, source_target_pairs={{0,4},{4,0},{8,12},{12,8},{16,20},{20,16},{24,28},{28,24},{1,5},{5... | collective-permute-start | bytes 798728 | tf_op jit(solution)/shard_map/ppermute | solution.py:384
  14.2 13.2 %collective-permute-start.3 = (f32[512,128]{1,0:T(8,128)S(1)}, f32[512,128]{1,0:T(8,128)S(1)}, u32[]{:S(2)}, u32[]{:S(2)}) collective-permute-start(f32[512,128]{1,0:T(8,128)S(1)} %shard_map.99.refs_2_), channel_id=1, source_target_pairs={{0,8},{4,12},{1,9},{5,13},{2,10},{6,14},{3,11},{7,15}} | collective-permute-start | bytes 786440 | tf_op jit(solution)/shard_map/ppermute | solution.py:397
  22.1 7.8 %collective-permute-start.2 = (f32[512,128]{1,0:T(8,128)S(1)}, f32[512,128]{1,0:T(8,128)S(1)}, u32[]{:S(2)}, u32[]{:S(2)}) collective-permute-start(f32[512,128]{1,0:T(8,128)S(1)} %shard_map.100.refs_4_), channel_id=1, source_target_pairs={{0,8},{4,12},{1,9},{5,13},{2,10},{6,14},{3,11},{7,15}} | collective-permute-start | bytes 786440 | tf_op jit(solution)/shard_map/ppermute | solution.py:397
  27.4 3.1 %copy-start.6 = (f32[16,512]{1,0:T(8,128)S(1)}, f32[16,512]{1,0:T(8,128)}, u32[]{:S(2)}) copy-start(f32[16,512]{1,0:T(8,128)} %get-tuple-element.54.refs_2_.refs_3_.refs_4_) | copy-start | bytes 98308
  27.5 5.0 %collective-permute-start.5 = (f32[512,128]{1,0:T(8,128)S(1)}, f32[512,128]{1,0:T(8,128)S(1)}, u32[]{:S(2)}, u32[]{:S(2)}) collective-permute-start(f32[512,128]{1,0:T(8,128)S(1)} %shard_map.102.refs_3_), channel_id=1, source_target_pairs={{8,16},{12,20},{9,17},{13,21},{10,18},{14,22},{11,19},{15,23}} | collective-permute-start | bytes 786440 | tf_op jit(solution)/shard_map/ppermute | solution.py:397
  29.8 3.3 %collective-permute-start.4 = (f32[512,128]{1,0:T(8,128)S(1)}, f32[512,128]{1,0:T(8,128)S(1)}, u32[]{:S(2)}, u32[]{:S(2)}) collective-permute-start(f32[512,128]{1,0:T(8,128)S(1)} %shard_map.103.refs_4_), channel_id=1, source_target_pairs={{8,16},{12,20},{9,17},{13,21},{10,18},{14,22},{11,19},{15,23}} | collective-permute-start | bytes 786440 | tf_op jit(solution)/shard_map/ppermute | solution.py:397
  32.5 3.3 %collective-permute-start.7 = (f32[512,128]{1,0:T(8,128)S(1)}, f32[512,128]{1,0:T(8,128)S(1)}, u32[]{:S(2)}, u32[]{:S(2)}) collective-permute-start(f32[512,128]{1,0:T(8,128)S(1)} %shard_map.105.refs_3_), channel_id=1, source_target_pairs={{16,24},{20,28},{17,25},{21,29},{18,26},{22,30},{19,27},{23,31}} | collective-permute-start | bytes 786440 | tf_op jit(solution)/shard_map/ppermute | solution.py:397
  33.2 5.3 %collective-permute-start.6 = (f32[512,128]{1,0:T(8,128)S(1)}, f32[512,128]{1,0:T(8,128)S(1)}, u32[]{:S(2)}, u32[]{:S(2)}) collective-permute-start(f32[512,128]{1,0:T(8,128)S(1)} %shard_map.106.refs_4_), channel_id=1, source_target_pairs={{16,24},{20,28},{17,25},{21,29},{18,26},{22,30},{19,27},{23,31}} | collective-permute-start | bytes 786440 | tf_op jit(solution)/shard_map/ppermute | solution.py:397
  35.8 1.6 %copy-start = (bf16[512,2048]{1,0:T(8,128)(2,1)S(1)}, bf16[512,2048]{1,0:T(8,128)(2,1)}, u32[]{:S(2)}) copy-start(bf16[512,2048]{1,0:T(8,128)(2,1)} %refs_1_.35) | copy-start | bytes 6291460
  35.8 1.6 %copy-start.7 = (f32[2048]{0:T(1024)S(1)}, f32[2048]{0:T(1024)}, u32[]{:S(2)}) copy-start(f32[2048]{0:T(1024)} %param.10) | copy-start | bytes 24580
  35.9 8.8 %collective-permute-start.9 = (f32[512,128]{1,0:T(8,128)S(1)}, f32[512,128]{1,0:T(8,128)S(1)}, u32[]{:S(2)}, u32[]{:S(2)}) collective-permute-start(f32[512,128]{1,0:T(8,128)S(1)} %get-tuple-element.57.refs_7_), channel_id=1, source_target_pairs={{0,4},{4,0},{8,12},{12,8},{16,20},{20,16},{24,28},{28,24},{1,5},{5... | collective-permute-start | bytes 786440 | tf_op jit(solution)/shard_map/ppermute | solution.py:409
  38.6 8.9 %collective-permute-start.8 = (f32[512,128]{1,0:T(8,128)S(1)}, f32[512,128]{1,0:T(8,128)S(1)}, u32[]{:S(2)}, u32[]{:S(2)}) collective-permute-start(f32[512,128]{1,0:T(8,128)S(1)} %get-tuple-element.60.refs_7_), channel_id=1, source_target_pairs={{0,4},{4,0},{8,12},{12,8},{16,20},{20,16},{24,28},{28,24},{1,5},{5... | collective-permute-start | bytes 786440 | tf_op jit(solution)/shard_map/ppermute | solution.py:409
  48.6 1.7 %collective-permute-start.12 = (f32[8,512]{1,0:T(8,128)S(1)}, f32[8,512]{1,0:T(8,128)S(1)}, u32[]{:S(2)}, u32[]{:S(2)}) collective-permute-start(f32[8,512]{1,0:T(8,128)S(1)} %get-tuple-element.64.refs_5_), channel_id=1, source_target_pairs={{0,3},{1,0},{2,1},{3,2},{4,7},{5,4},{6,5},{7,6},{8,11},{9,8},{10,9... | collective-permute-start | bytes 49160 | tf_op jit(solution)/shard_map/ppermute | solution.py:476
  48.6 3.8 %collective-permute-start.11 = (f32[8,512]{1,0:T(8,128)S(1)}, f32[8,512]{1,0:T(8,128)S(1)}, u32[]{:S(2)}, u32[]{:S(2)}) collective-permute-start(f32[8,512]{1,0:T(8,128)S(1)} %get-tuple-element.64.refs_5_), channel_id=1, source_target_pairs={{0,2},{1,3},{2,0},{3,1},{4,6},{5,7},{6,4},{7,5},{8,10},{9,11},{10,... | collective-permute-start | bytes 49160 | tf_op jit(solution)/shard_map/ppermute | solution.py:476
  50.2 3.2 %collective-permute-start.10 = (f32[8,512]{1,0:T(8,128)S(1)}, f32[8,512]{1,0:T(8,128)S(1)}, u32[]{:S(2)}, u32[]{:S(2)}) collective-permute-start(f32[8,512]{1,0:T(8,128)S(1)} %get-tuple-element.64.refs_5_), channel_id=1, source_target_pairs={{0,1},{1,2},{2,3},{3,0},{4,5},{5,6},{6,7},{7,4},{8,9},{9,10},{10,1... | collective-permute-start | bytes 49160 | tf_op jit(solution)/shard_map/ppermute | solution.py:476
  55.1 7.3 %collective-permute-start.14 = (f32[520,128]{1,0:T(8,128)S(1)}, f32[520,128]{1,0:T(8,128)S(1)}, u32[]{:S(2)}, u32[]{:S(2)}) collective-permute-start(f32[520,128]{1,0:T(8,128)S(1)} %get-tuple-element.69.refs_10_), channel_id=1, source_target_pairs={{0,4},{4,0},{8,12},{12,8},{16,20},{20,16},{24,28},{28,24},{1,5},{5... | collective-permute-start | bytes 798728 | tf_op jit(solution)/shard_map/ppermute | solution.py:381
  60.7 6.9 %collective-permute-start.13 = (f32[520,128]{1,0:T(8,128)S(1)}, f32[520,128]{1,0:T(8,128)S(1)}, u32[]{:S(2)}, u32[]{:S(2)}) collective-permute-start(f32[520,128]{1,0:T(8,128)S(1)} %shard_map.118.refs_2_), channel_id=1, source_target_pairs={{0,4},{4,0},{8,12},{12,8},{16,20},{20,16},{24,28},{28,24},{1,5},{5... | collective-permute-start | bytes 798728 | tf_op jit(solution)/shard_map/ppermute | solution.py:384
  62.3 9.9 %collective-permute-start.16 = (f32[512,128]{1,0:T(8,128)S(1)}, f32[512,128]{1,0:T(8,128)S(1)}, u32[]{:S(2)}, u32[]{:S(2)}) collective-permute-start(f32[512,128]{1,0:T(8,128)S(1)} %shard_map.119.refs_2_), channel_id=1, source_target_pairs={{24,16},{28,20},{25,17},{29,21},{26,18},{30,22},{27,19},{31,23}} | collective-permute-start | bytes 786440 | tf_op jit(solution)/shard_map/ppermute | solution.py:397
  67.6 5.3 %collective-permute-start.15 = (f32[512,128]{1,0:T(8,128)S(1)}, f32[512,128]{1,0:T(8,128)S(1)}, u32[]{:S(2)}, u32[]{:S(2)}) collective-permute-start(f32[512,128]{1,0:T(8,128)S(1)} %shard_map.120.refs_6_), channel_id=1, source_target_pairs={{24,16},{28,20},{25,17},{29,21},{26,18},{30,22},{27,19},{31,23}} | collective-permute-start | bytes 786440 | tf_op jit(solution)/shard_map/ppermute | solution.py:397
  72.2 9.3 %collective-permute-start.18 = (f32[512,128]{1,0:T(8,128)S(1)}, f32[512,128]{1,0:T(8,128)S(1)}, u32[]{:S(2)}, u32[]{:S(2)}) collective-permute-start(f32[512,128]{1,0:T(8,128)S(1)} %shard_map.122.refs_3_), channel_id=1, source_target_pairs={{16,8},{20,12},{17,9},{21,13},{18,10},{22,14},{19,11},{23,15}} | collective-permute-start | bytes 786440 | tf_op jit(solution)/shard_map/ppermute | solution.py:397
  72.9 9.9 %collective-permute-start.17 = (f32[512,128]{1,0:T(8,128)S(1)}, f32[512,128]{1,0:T(8,128)S(1)}, u32[]{:S(2)}, u32[]{:S(2)}) collective-permute-start(f32[512,128]{1,0:T(8,128)S(1)} %shard_map.123.refs_7_), channel_id=1, source_target_pairs={{16,8},{20,12},{17,9},{21,13},{18,10},{22,14},{19,11},{23,15}} | collective-permute-start | bytes 786440 | tf_op jit(solution)/shard_map/ppermute | solution.py:397
  81.5 19.1 %collective-permute-start.20 = (f32[512,128]{1,0:T(8,128)S(1)}, f32[512,128]{1,0:T(8,128)S(1)}, u32[]{:S(2)}, u32[]{:S(2)}) collective-permute-start(f32[512,128]{1,0:T(8,128)S(1)} %shard_map.126.refs_3_), channel_id=1, source_target_pairs={{8,0},{12,4},{9,1},{13,5},{10,2},{14,6},{11,3},{15,7}} | collective-permute-start | bytes 786440 | tf_op jit(solution)/shard_map/ppermute | solution.py:397
  82.8 20.6 %collective-permute-start.19 = (f32[512,128]{1,0:T(8,128)S(1)}, f32[512,128]{1,0:T(8,128)S(1)}, u32[]{:S(2)}, u32[]{:S(2)}) collective-permute-start(f32[512,128]{1,0:T(8,128)S(1)} %shard_map.127.refs_7_), channel_id=1, source_target_pairs={{8,0},{12,4},{9,1},{13,5},{10,2},{14,6},{11,3},{15,7}} | collective-permute-start | bytes 786440 | tf_op jit(solution)/shard_map/ppermute | solution.py:397
  100.6 8.4 %collective-permute-start.22 = (f32[512,128]{1,0:T(8,128)S(1)}, f32[512,128]{1,0:T(8,128)S(1)}, u32[]{:S(2)}, u32[]{:S(2)}) collective-permute-start(f32[512,128]{1,0:T(8,128)S(1)} %get-tuple-element.89.refs_5_), channel_id=1, source_target_pairs={{0,4},{4,0},{8,12},{12,8},{16,20},{20,16},{24,28},{28,24},{1,5},{5... | collective-permute-start | bytes 786440 | tf_op jit(solution)/shard_map/ppermute | solution.py:409
  103.5 8.4 %collective-permute-start.21 = (f32[512,128]{1,0:T(8,128)S(1)}, f32[512,128]{1,0:T(8,128)S(1)}, u32[]{:S(2)}, u32[]{:S(2)}) collective-permute-start(f32[512,128]{1,0:T(8,128)S(1)} %get-tuple-element.90.refs_6_), channel_id=1, source_target_pairs={{0,4},{4,0},{8,12},{12,8},{16,20},{20,16},{24,28},{28,24},{1,5},{5... | collective-permute-start | bytes 786440 | tf_op jit(solution)/shard_map/ppermute | solution.py:409
